TPU v7x, 32 devices: a whole 2x2x4 slice. The times are simulated.
32 devices in a mesh: gx: 2 (over y), gy: 4 (over x, core), gz: 4 (over z).
Axes of the slice: x: 2, y: 2, z: 4, core: 2. Of those that a mesh axis runs over, the one named last changes fastest.
Arguments:
- fill_mask: int32 [32, 32, 512], P('gx', 'gy', 'gz'), may hold values from 0 to 1, as said below
- membrane_flags: int32 [32, 32, 512], P('gx', 'gy', 'gz'), may hold values from 0 to 1, as said below
- smear: float32 [32, 32, 512], P('gx', 'gy', 'gz'), may hold values from 0 to 1, as said below
- velocity: float32 [3, 32, 32, 512], P(None, 'gx', 'gy', 'gz'), may hold values from -6 to 6
Outputs:
- velocity_out: float32 [3, 32, 32, 512], P(None, 'gx', 'gy', 'gz')
- fraction_out: float32 [32, 32, 512], P('gx', 'gy', 'gz')
Inputs may be any that keep to these rules, and one draw needn't show every extreme that they name: In every column along the height, fill_mask is 1 below a surface height and 0 above it; the surface lies strictly inside the tank. membrane_flags is nonzero only on the four planes across the length at positions 4 + k * 8. smear is nonzero only on the two cells of each column next to its liquid surface.
All inputs are finite; a program needn't handle non-finite values.
Results may differ from a plain program's by a relative error of at most 0.0003.
Values sent between devices are 32-bit elements; how exact they have to be, the bound alone decides.
A program may use at most 128 MiB of HBM per device.

v0:
```python
import jax
import jax.numpy as jnp
from jax import lax
from jax.sharding import PartitionSpec as P

LEVELS = 4
COARSE_SWEEPS = 8


RHO_LIQUID = 1000.0
RHO_GAS = 1.0
MEMBRANE_DROP = 49.0
SIGMA_SHIFT = 0.1
OMEGA = 0.8
TIME_STEP = 0.2


def extended(block, sides, width):
    for axis, dim in sides:
        count = lax.axis_size(axis)
        forward = [(i, i + 1) for i in range(count - 1)]
        backward = [(target, source) for source, target in forward]
        low = lax.ppermute(
            lax.slice_in_dim(block, block.shape[dim] - width, None, axis=dim), axis, forward
        )
        high = lax.ppermute(lax.slice_in_dim(block, 0, width, axis=dim), axis, backward)
        block = jnp.concatenate([low, block, high], axis=dim)
    return block


def phase_fields(fill_mask, membrane_flags, smear):
    filled = fill_mask.astype(jnp.float32)
    walled = membrane_flags.astype(jnp.float32)
    fraction = filled * (1.0 - 0.4 * smear) + (1.0 - filled) * (0.4 * smear)
    density = RHO_GAS + (RHO_LIQUID - RHO_GAS) * fraction
    conductance = 1.0 / (density * (1.0 + MEMBRANE_DROP * walled))
    return (fraction, conductance)


def harmonic(lower_value, upper_value):
    return 2.0 * lower_value * upper_value / (lower_value + upper_value)


def fine_tables(padded):
    center = padded[1:-1, 1:-1, 1:-1]
    upper_faces = [
        harmonic(center, padded[2:, 1:-1, 1:-1]),
        harmonic(center, padded[1:-1, 2:, 1:-1]),
        harmonic(center, padded[1:-1, 1:-1, 2:]),
    ]
    lower_faces = [
        harmonic(padded[:-2, 1:-1, 1:-1], center),
        harmonic(padded[1:-1, :-2, 1:-1], center),
        harmonic(padded[1:-1, 1:-1, :-2], center),
    ]
    return (upper_faces, lower_faces, SIGMA_SHIFT * center)


def with_diagonal(upper_faces, lower_faces, shift_term):
    diagonal = (
        shift_term
        + upper_faces[0]
        + lower_faces[0]
        + upper_faces[1]
        + lower_faces[1]
        + upper_faces[2]
        + lower_faces[2]
    )
    return (upper_faces, lower_faces, diagonal)


def blocks(field):
    shape = field.shape
    return field.reshape(shape[0] // 2, 2, shape[1] // 2, 2, shape[2] // 2, 2)


def coarsen_tables(upper_faces, lower_faces, shift_term):
    upper_new = [
        blocks(upper_faces[0])[:, 1].sum(axis=(2, 4)),
        blocks(upper_faces[1])[:, :, :, 1].sum(axis=(1, 4)),
        blocks(upper_faces[2])[..., 1].sum(axis=(1, 3)),
    ]
    lower_new = [
        blocks(lower_faces[0])[:, 0].sum(axis=(2, 4)),
        blocks(lower_faces[1])[:, :, :, 0].sum(axis=(1, 4)),
        blocks(lower_faces[2])[..., 0].sum(axis=(1, 3)),
    ]
    return (upper_new, lower_new, blocks(shift_term).sum(axis=(1, 3, 5)))


def restrict(field):
    return blocks(field).sum(axis=(1, 3, 5))


def prolong(field):
    shape = field.shape
    wide = jnp.broadcast_to(
        field[:, None, :, None, :, None], (shape[0], 2, shape[1], 2, shape[2], 2)
    )
    return wide.reshape(2 * shape[0], 2 * shape[1], 2 * shape[2])


def apply_padded(padded, tables):
    upper_faces, lower_faces, diagonal = tables
    center = padded[1:-1, 1:-1, 1:-1]
    total = diagonal * center
    total = total - (
        upper_faces[0] * padded[2:, 1:-1, 1:-1] + lower_faces[0] * padded[:-2, 1:-1, 1:-1]
    )
    total = total - (
        upper_faces[1] * padded[1:-1, 2:, 1:-1] + lower_faces[1] * padded[1:-1, :-2, 1:-1]
    )
    total = total - (
        upper_faces[2] * padded[1:-1, 1:-1, 2:] + lower_faces[2] * padded[1:-1, 1:-1, :-2]
    )
    return total


def jacobi_sweep(padded, right_side, tables):
    center = padded[1:-1, 1:-1, 1:-1]
    return center + OMEGA * (right_side - apply_padded(padded, tables)) / tables[2]


def with_rims(field):
    return extended(field, (("gx", 0), ("gy", 1), ("gz", 2)), 1)


def after_rims(field):
    return extended(field, (("gx", 0), ("gy", 1), ("gz", 2)), 1)


def shards(fill_mask, membrane_flags, smear, velocity):
    fraction, conductance = phase_fields(fill_mask, membrane_flags, smear)
    shape = fraction.shape
    counts = (lax.axis_size("gx"), lax.axis_size("gy"), lax.axis_size("gz"))
    offsets = (lax.axis_index("gx"), lax.axis_index("gy"), lax.axis_index("gz"))
    open_velocity = []
    for axis_dim in range(3):
        first_cell = offsets[axis_dim] * shape[axis_dim]
        ramp = first_cell + jnp.arange(shape[axis_dim]) < shape[axis_dim] * counts[axis_dim] - 1
        view = [1, 1, 1]
        view[axis_dim] = shape[axis_dim]
        open_velocity.append(velocity[axis_dim] * ramp.astype(jnp.float32).reshape(view))
    stacked = jnp.stack(
        [conductance, fraction, open_velocity[0], open_velocity[1], open_velocity[2]]
    )
    rims = extended(stacked, (("gx", 1), ("gy", 2), ("gz", 3)), 1)
    frac_pad = rims[1]
    upper_faces, lower_faces, shift_term = fine_tables(rims[0])
    levels = []
    for level in range(LEVELS):
        levels.append(with_diagonal(upper_faces, lower_faces, shift_term))
        if level < LEVELS - 1:
            upper_faces, lower_faces, shift_term = coarsen_tables(
                upper_faces, lower_faces, shift_term
            )
    velocity_low = [rims[2][:-2, 1:-1, 1:-1], rims[3][1:-1, :-2, 1:-1], rims[4][1:-1, 1:-1, :-2]]
    right_side = -(
        open_velocity[0]
        - velocity_low[0]
        + (open_velocity[1] - velocity_low[1])
        + (open_velocity[2] - velocity_low[2])
    )

    def coarsest_solve(rhs, tables):
        pressure = jacobi_sweep(jnp.pad(jnp.zeros_like(rhs), 1), rhs, tables)
        for _ in range(COARSE_SWEEPS - 1):
            padded = extended(pressure, (("gx", 0), ("gy", 1), ("gz", 2)), 1)
            pressure = jacobi_sweep(padded, rhs, tables)
        return pressure

    def vcycle_level(level, rhs):
        tables = levels[level]
        if level == LEVELS - 1:
            return coarsest_solve(rhs, tables)
        pressure = jacobi_sweep(jnp.pad(jnp.zeros_like(rhs), 1), rhs, tables)
        pressure = jacobi_sweep(with_rims(pressure), rhs, tables)
        residual = rhs - apply_padded(with_rims(pressure), tables)
        pressure = pressure + prolong(vcycle_level(level + 1, restrict(residual)))
        for _ in range(2):
            pressure = jacobi_sweep(after_rims(pressure), rhs, tables)
        return pressure

    pressure = vcycle_level(0, right_side)
    padded = extended(pressure, (("gx", 0), ("gy", 1), ("gz", 2)), 1)
    upper_zero, lower_zero = (levels[0][0], levels[0][1])
    above = [padded[2:, 1:-1, 1:-1], padded[1:-1, 2:, 1:-1], padded[1:-1, 1:-1, 2:]]
    beneath = [padded[:-2, 1:-1, 1:-1], padded[1:-1, :-2, 1:-1], padded[1:-1, 1:-1, :-2]]
    frac_up = [frac_pad[2:, 1:-1, 1:-1], frac_pad[1:-1, 2:, 1:-1], frac_pad[1:-1, 1:-1, 2:]]
    frac_down = [frac_pad[:-2, 1:-1, 1:-1], frac_pad[1:-1, :-2, 1:-1], frac_pad[1:-1, 1:-1, :-2]]
    new_velocity = []
    change = jnp.zeros_like(fraction)
    for axis_dim in range(3):
        moved = open_velocity[axis_dim] - upper_zero[axis_dim] * (above[axis_dim] - pressure)
        moved_low = velocity_low[axis_dim] - lower_zero[axis_dim] * (pressure - beneath[axis_dim])
        new_velocity.append(moved)
        flux = moved * jnp.where(moved > 0, fraction, frac_up[axis_dim])
        flux_low = moved_low * jnp.where(moved_low > 0, frac_down[axis_dim], fraction)
        change = change + (flux - flux_low)
    fraction_out = fraction - TIME_STEP * change
    return (jnp.stack(new_velocity), fraction_out)


def solution(mesh):
    placed = (
        P("gx", "gy", "gz"),
        P("gx", "gy", "gz"),
        P("gx", "gy", "gz"),
        P(None, "gx", "gy", "gz"),
    )
    return jax.shard_map(
        shards,
        mesh=mesh,
        in_specs=placed,
        out_specs=(P(None, "gx", "gy", "gz"), P("gx", "gy", "gz")),
        check_vma=False,
    )
```

profile of v0, /device:TPU:1, one launch (start us, length us, event | category | flops | bytes accessed | tf_op | source)
XLA Modules:
  0.0 543.1 jit_solution(10251998255911368508)
XLA Ops:
  13.8 5.1 collective-permute-start.2
  36.2 5.5 %reshape.221 = f32[8,2,4,2,64,2]{5,4,3,2,1,0:T(8,128)} reshape(f32[16,8,128]{2,1,0:T(8,128)S(1)} %get-tuple-element.11) | data formatting | bytes 131072 | tf_op jit(solution)/shard_map/reshape | solution.py:74
  41.7 5.5 %reshape.222 = f32[8,2,4,2,64,2]{5,4,3,2,1,0:T(8,128)} reshape(f32[16,8,128]{2,1,0:T(8,128)S(1)} %get-tuple-element.5) | data formatting | bytes 131072 | tf_op jit(solution)/shard_map/reshape | solution.py:74
  47.2 5.6 %reshape.219 = f32[8,2,4,2,64,2]{5,4,3,2,1,0:T(8,128)} reshape(f32[16,8,128]{2,1,0:T(8,128)S(1)} %get-tuple-element.7) | data formatting | bytes 131072 | tf_op jit(solution)/shard_map/reshape | solution.py:74
  52.8 5.5 %reshape.220 = f32[8,2,4,2,64,2]{5,4,3,2,1,0:T(8,128)} reshape(f32[16,8,128]{2,1,0:T(8,128)S(1)} %get-tuple-element.6) | data formatting | bytes 131072 | tf_op jit(solution)/shard_map/reshape | solution.py:74
  59.6 4.4 collective-permute-start.7
  64.0 5.2 slice_reduce_fusion
  69.9 5.6 %reshape.217 = f32[8,2,4,2,64,2]{5,4,3,2,1,0:T(8,128)} reshape(f32[16,8,128]{2,1,0:T(8,128)S(1)} %get-tuple-element.9) | data formatting | bytes 131072 | tf_op jit(solution)/shard_map/reshape | solution.py:74
  75.5 5.5 %reshape.218 = f32[8,2,4,2,64,2]{5,4,3,2,1,0:T(8,128)} reshape(f32[16,8,128]{2,1,0:T(8,128)S(1)} %get-tuple-element.8) | data formatting | bytes 131072 | tf_op jit(solution)/shard_map/reshape | solution.py:74
  91.2 4.0 collective-permute-start.11
  100.5 4.0 collective-permute-start.13
  113.9 5.4 collective-permute-start.17
  119.4 5.5 %reshape.216 = f32[8,2,4,2,64,2]{5,4,3,2,1,0:T(8,128)} reshape(f32[16,8,128]{2,1,0:T(8,128)S(1)} %get-tuple-element.24) | data formatting | bytes 131072 | tf_op jit(solution)/shard_map/reshape | solution.py:74
  129.3 5.5 %reshape.215 = f32[8,2,4,2,64,2]{5,4,3,2,1,0:T(8,128)} reshape(f32[16,8,128]{2,1,0:T(8,128)S(1)} %fusion.81) | data formatting | bytes 131072 | tf_op jit(solution)/shard_map/reshape | solution.py:74
  138.8 4.0 collective-permute-start.19
  146.2 4.9 collective-permute-start.21
  153.3 4.0 collective-permute-start.23
  159.8 4.0 collective-permute-start.25
  166.5 6.4 %collective-permute-start.27 = (f32[10,1,64]{2,1,0:T(1,128)S(1)}, f32[10,1,64]{2,1,0:T(1,128)S(1)}, u32[]{:S(2)}, u32[]{:S(2)}) collective-permute-start(f32[10,1,64]{2,1,0:T(1,128)S(1)} %get-tuple-element.69), channel_id=1, source_target_pairs={{0,4},{4,8},{8,12},{1,5},{5,9},{9,13},{2,6},{6,10},{10,14},{3,7},{... | collective-permute-start | bytes 7688 | tf_op jit(solution)/shard_map/ppermute | solution.py:23
  175.1 4.6 collective-permute-start.29
  183.0 4.0 collective-permute-start.31
  189.6 6.2 %collective-permute-start.33 = (f32[6,1,32]{2,0,1:T(8,128)S(1)}, f32[6,1,32]{2,0,1:T(8,128)S(1)}, u32[]{:S(2)}, u32[]{:S(2)}) collective-permute-start(f32[6,1,32]{2,0,1:T(8,128)S(1)} %get-tuple-element.95), channel_id=1, source_target_pairs={{0,4},{4,8},{8,12},{1,5},{5,9},{9,13},{2,6},{6,10},{10,14},{3,7},{... | collective-permute-start | bytes 2312 | tf_op jit(solution)/shard_map/ppermute | solution.py:23
  197.9 4.6 collective-permute-start.35
  204.7 4.0 collective-permute-start.37
  211.4 6.2 %collective-permute-start.39 = (f32[6,1,32]{2,0,1:T(8,128)S(1)}, f32[6,1,32]{2,0,1:T(8,128)S(1)}, u32[]{:S(2)}, u32[]{:S(2)}) collective-permute-start(f32[6,1,32]{2,0,1:T(8,128)S(1)} %get-tuple-element.93), channel_id=1, source_target_pairs={{0,4},{4,8},{8,12},{1,5},{5,9},{9,13},{2,6},{6,10},{10,14},{3,7},{... | collective-permute-start | bytes 2312 | tf_op jit(solution)/shard_map/ppermute | solution.py:23
  220.1 4.5 collective-permute-start.41
  227.2 4.0 collective-permute-start.43
  233.8 5.7 %collective-permute-start.45 = (f32[4,1,16]{2,0,1:T(4,128)S(1)}, f32[4,1,16]{2,0,1:T(4,128)S(1)}, u32[]{:S(2)}, u32[]{:S(2)}) collective-permute-start(f32[4,1,16]{2,0,1:T(4,128)S(1)} %pad_maximum_fusion.293), channel_id=1, source_target_pairs={{0,4},{4,8},{8,12},{1,5},{5,9},{9,13},{2,6},{6,10},{10,14},{3,7},{... | collective-permute-start | bytes 776 | tf_op jit(solution)/shard_map/ppermute | solution.py:23
  241.6 4.5 collective-permute-start.47
  248.3 4.0 collective-permute-start.49
  255.0 6.2 %collective-permute-start.51 = (f32[4,1,16]{2,0,1:T(4,128)S(1)}, f32[4,1,16]{2,0,1:T(4,128)S(1)}, u32[]{:S(2)}, u32[]{:S(2)}) collective-permute-start(f32[4,1,16]{2,0,1:T(4,128)S(1)} %pad_maximum_fusion.296), channel_id=1, source_target_pairs={{0,4},{4,8},{8,12},{1,5},{5,9},{9,13},{2,6},{6,10},{10,14},{3,7},{... | collective-permute-start | bytes 776 | tf_op jit(solution)/shard_map/ppermute | solution.py:23
  263.2 4.5 collective-permute-start.53
  269.9 4.0 collective-permute-start.55
  276.6 6.2 %collective-permute-start.57 = (f32[4,1,16]{2,0,1:T(4,128)S(1)}, f32[4,1,16]{2,0,1:T(4,128)S(1)}, u32[]{:S(2)}, u32[]{:S(2)}) collective-permute-start(f32[4,1,16]{2,0,1:T(4,128)S(1)} %pad_maximum_fusion.299), channel_id=1, source_target_pairs={{0,4},{4,8},{8,12},{1,5},{5,9},{9,13},{2,6},{6,10},{10,14},{3,7},{... | collective-permute-start | bytes 776 | tf_op jit(solution)/shard_map/ppermute | solution.py:23
  284.8 4.5 collective-permute-start.59
  291.5 4.0 collective-permute-start.61
  298.1 6.2 %collective-permute-start.63 = (f32[4,1,16]{2,0,1:T(4,128)S(1)}, f32[4,1,16]{2,0,1:T(4,128)S(1)}, u32[]{:S(2)}, u32[]{:S(2)}) collective-permute-start(f32[4,1,16]{2,0,1:T(4,128)S(1)} %pad_maximum_fusion.302), channel_id=1, source_target_pairs={{0,4},{4,8},{8,12},{1,5},{5,9},{9,13},{2,6},{6,10},{10,14},{3,7},{... | collective-permute-start | bytes 776 | tf_op jit(solution)/shard_map/ppermute | solution.py:23
  306.4 4.5 collective-permute-start.65
  313.1 4.0 collective-permute-start.67
  319.7 6.2 %collective-permute-start.69 = (f32[4,1,16]{2,0,1:T(4,128)S(1)}, f32[4,1,16]{2,0,1:T(4,128)S(1)}, u32[]{:S(2)}, u32[]{:S(2)}) collective-permute-start(f32[4,1,16]{2,0,1:T(4,128)S(1)} %pad_maximum_fusion.305), channel_id=1, source_target_pairs={{0,4},{4,8},{8,12},{1,5},{5,9},{9,13},{2,6},{6,10},{10,14},{3,7},{... | collective-permute-start | bytes 776 | tf_op jit(solution)/shard_map/ppermute | solution.py:23
  328.0 4.5 collective-permute-start.71
  334.7 4.0 collective-permute-start.73
  341.3 6.2 %collective-permute-start.75 = (f32[4,1,16]{2,0,1:T(4,128)S(1)}, f32[4,1,16]{2,0,1:T(4,128)S(1)}, u32[]{:S(2)}, u32[]{:S(2)}) collective-permute-start(f32[4,1,16]{2,0,1:T(4,128)S(1)} %pad_maximum_fusion.308), channel_id=1, source_target_pairs={{0,4},{4,8},{8,12},{1,5},{5,9},{9,13},{2,6},{6,10},{10,14},{3,7},{... | collective-permute-start | bytes 776 | tf_op jit(solution)/shard_map/ppermute | solution.py:23
  349.6 4.5 collective-permute-start.77
  356.3 4.0 collective-permute-start.79
  362.9 6.2 %collective-permute-start.81 = (f32[4,1,16]{2,0,1:T(4,128)S(1)}, f32[4,1,16]{2,0,1:T(4,128)S(1)}, u32[]{:S(2)}, u32[]{:S(2)}) collective-permute-start(f32[4,1,16]{2,0,1:T(4,128)S(1)} %pad_maximum_fusion.311), channel_id=1, source_target_pairs={{0,4},{4,8},{8,12},{1,5},{5,9},{9,13},{2,6},{6,10},{10,14},{3,7},{... | collective-permute-start | bytes 776 | tf_op jit(solution)/shard_map/ppermute | solution.py:23
  371.2 4.5 collective-permute-start.83
  384.7 6.2 %collective-permute-start.87 = (f32[6,1,32]{2,0,1:T(8,128)S(1)}, f32[6,1,32]{2,0,1:T(8,128)S(1)}, u32[]{:S(2)}, u32[]{:S(2)}) collective-permute-start(f32[6,1,32]{2,0,1:T(8,128)S(1)} %get-tuple-element.91), channel_id=1, source_target_pairs={{0,4},{4,8},{8,12},{1,5},{5,9},{9,13},{2,6},{6,10},{10,14},{3,7},{... | collective-permute-start | bytes 2312 | tf_op jit(solution)/shard_map/ppermute | solution.py:23
  393.0 4.5 collective-permute-start.89
  406.4 6.2 %collective-permute-start.93 = (f32[6,1,32]{2,0,1:T(8,128)S(1)}, f32[6,1,32]{2,0,1:T(8,128)S(1)}, u32[]{:S(2)}, u32[]{:S(2)}) collective-permute-start(f32[6,1,32]{2,0,1:T(8,128)S(1)} %get-tuple-element.89), channel_id=1, source_target_pairs={{0,4},{4,8},{8,12},{1,5},{5,9},{9,13},{2,6},{6,10},{10,14},{3,7},{... | collective-permute-start | bytes 2312 | tf_op jit(solution)/shard_map/ppermute | solution.py:23
  414.7 4.5 collective-permute-start.95
  428.6 6.2 %collective-permute-start.99 = (f32[10,1,64]{2,1,0:T(1,128)S(1)}, f32[10,1,64]{2,1,0:T(1,128)S(1)}, u32[]{:S(2)}, u32[]{:S(2)}) collective-permute-start(f32[10,1,64]{2,1,0:T(1,128)S(1)} %get-tuple-element.67), channel_id=1, source_target_pairs={{0,4},{4,8},{8,12},{1,5},{5,9},{9,13},{2,6},{6,10},{10,14},{3,7},{... | collective-permute-start | bytes 7688 | tf_op jit(solution)/shard_map/ppermute | solution.py:23
  436.9 4.5 collective-permute-start.101
  450.6 6.2 %collective-permute-start.105 = (f32[10,1,64]{2,1,0:T(1,128)S(1)}, f32[10,1,64]{2,1,0:T(1,128)S(1)}, u32[]{:S(2)}, u32[]{:S(2)}) collective-permute-start(f32[10,1,64]{2,1,0:T(1,128)S(1)} %get-tuple-element.65), channel_id=1, source_target_pairs={{0,4},{4,8},{8,12},{1,5},{5,9},{9,13},{2,6},{6,10},{10,14},{3,7},{... | collective-permute-start | bytes 7688 | tf_op jit(solution)/shard_map/ppermute | solution.py:23
  459.0 4.6 collective-permute-start.107
  467.4 4.0 reshape.238
  472.7 4.0 collective-permute-start.109
  479.4 6.2 %collective-permute-start.111 = (f32[18,1,128]{2,1,0:T(1,128)S(1)}, f32[18,1,128]{2,1,0:T(1,128)S(1)}, u32[]{:S(2)}, u32[]{:S(2)}) collective-permute-start(f32[18,1,128]{2,1,0:T(1,128)S(1)} %get-tuple-element.41), channel_id=1, source_target_pairs={{0,4},{4,8},{8,12},{1,5},{5,9},{9,13},{2,6},{6,10},{10,14},{3,7},{... | collective-permute-start | bytes 27656 | tf_op jit(solution)/shard_map/ppermute | solution.py:23
  487.9 4.7 collective-permute-start.113
  502.8 6.2 %collective-permute-start.117 = (f32[18,1,128]{2,1,0:T(1,128)S(1)}, f32[18,1,128]{2,1,0:T(1,128)S(1)}, u32[]{:S(2)}, u32[]{:S(2)}) collective-permute-start(f32[18,1,128]{2,1,0:T(1,128)S(1)} %get-tuple-element.39), channel_id=1, source_target_pairs={{0,4},{4,8},{8,12},{1,5},{5,9},{9,13},{2,6},{6,10},{10,14},{3,7},{... | collective-permute-start | bytes 27656 | tf_op jit(solution)/shard_map/ppermute | solution.py:23
  511.2 4.7 collective-permute-start.119
  519.5 4.0 collective-permute-start.121
  526.2 6.2 %collective-permute-start.123 = (f32[18,1,128]{2,1,0:T(1,128)S(1)}, f32[18,1,128]{2,1,0:T(1,128)S(1)}, u32[]{:S(2)}, u32[]{:S(2)}) collective-permute-start(f32[18,1,128]{2,1,0:T(1,128)S(1)} %get-tuple-element.37), channel_id=1, source_target_pairs={{0,4},{4,8},{8,12},{1,5},{5,9},{9,13},{2,6},{6,10},{10,14},{3,7},{... | collective-permute-start | bytes 27656 | tf_op jit(solution)/shard_map/ppermute | solution.py:23
  534.6 4.7 collective-permute-start.125
  (433 shorter events, 220.3 us)
Async XLA Ops:
  13.8 7.0 %collective-permute-start.2 = (f32[5,18,1,128]{3,2,1,0:T(1,128)S(1)}, f32[5,18,1,128]{3,2,1,0:T(1,128)S(1)}, u32[]{:S(2)}, u32[]{:S(2)}) collective-permute-start(f32[5,18,1,128]{3,2,1,0:T(1,128)S(1)} %get-tuple-element.19), channel_id=1, source_target_pairs={{0,4},{4,8},{8,12},{1,5},{5,9},{9,13},{2,6},{6,10},{10,14},{3,7},{... | collective-permute-start | bytes 138248 | tf_op jit(solution)/shard_map/ppermute | solution.py:23
  58.3 22.7 %collective-permute-start.6 = (f32[1,8,128]{2,1,0:T(8,128)S(1)}, f32[1,8,128]{2,1,0:T(8,128)S(1)}, u32[]{:S(2)}, u32[]{:S(2)}) collective-permute-start(f32[1,8,128]{2,1,0:T(8,128)S(1)} %get-tuple-element.56), channel_id=1, source_target_pairs={{16,0},{17,1},{18,2},{19,3},{20,4},{21,5},{22,6},{23,7},{24,8},{25... | collective-permute-start | bytes 12296 | tf_op jit(solution)/shard_map/ppermute | solution.py:26
  59.6 21.4 %collective-permute-start.7 = (f32[1,8,128]{2,1,0:T(8,128)S(1)}, f32[1,8,128]{2,1,0:T(8,128)S(1)}, u32[]{:S(2)}, u32[]{:S(2)}) collective-permute-start(f32[1,8,128]{2,1,0:T(8,128)S(1)} %get-tuple-element.55), channel_id=1, source_target_pairs={{0,16},{1,17},{2,18},{3,19},{4,20},{5,21},{6,22},{7,23},{8,24},{9,... | collective-permute-start | bytes 12296 | tf_op jit(solution)/shard_map/ppermute | solution.py:23
  81.0 8.7 %collective-permute-start.8 = (f32[18,1,128]{2,1,0:T(1,128)S(1)}, f32[18,1,128]{2,1,0:T(1,128)S(1)}, u32[]{:S(2)}, u32[]{:S(2)}) collective-permute-start(f32[18,1,128]{2,1,0:T(1,128)S(1)} %get-tuple-element.46), channel_id=1, source_target_pairs={{4,0},{8,4},{12,8},{5,1},{9,5},{13,9},{6,2},{10,6},{14,10},{7,3},{... | collective-permute-start | bytes 27656 | tf_op jit(solution)/shard_map/ppermute | solution.py:26
  83.0 6.8 %collective-permute-start.9 = (f32[18,1,128]{2,1,0:T(1,128)S(1)}, f32[18,1,128]{2,1,0:T(1,128)S(1)}, u32[]{:S(2)}, u32[]{:S(2)}) collective-permute-start(f32[18,1,128]{2,1,0:T(1,128)S(1)} %get-tuple-element.45), channel_id=1, source_target_pairs={{0,4},{4,8},{8,12},{1,5},{5,9},{9,13},{2,6},{6,10},{10,14},{3,7},{... | collective-permute-start | bytes 27656 | tf_op jit(solution)/shard_map/ppermute | solution.py:23
  89.9 6.5 %collective-permute-start.10 = (f32[18,10,1]{2,1,0:T(8,128)S(1)}, f32[18,10,1]{2,1,0:T(8,128)S(1)}, u32[]{:S(2)}, u32[]{:S(2)}) collective-permute-start(f32[18,10,1]{2,1,0:T(8,128)S(1)} %get-tuple-element.35), channel_id=1, source_target_pairs={{1,0},{2,1},{3,2},{5,4},{6,5},{7,6},{9,8},{10,9},{11,10},{13,12},{... | collective-permute-start | bytes 2168 | tf_op jit(solution)/shard_map/ppermute | solution.py:26
  91.2 6.9 %collective-permute-start.11 = (f32[18,10,1]{2,1,0:T(8,128)S(1)}, f32[18,10,1]{2,1,0:T(8,128)S(1)}, u32[]{:S(2)}, u32[]{:S(2)}) collective-permute-start(f32[18,10,1]{2,1,0:T(8,128)S(1)} %get-tuple-element.36), channel_id=1, source_target_pairs={{0,1},{1,2},{2,3},{4,5},{5,6},{6,7},{8,9},{9,10},{10,11},{12,13},{... | collective-permute-start | bytes 2168 | tf_op jit(solution)/shard_map/ppermute | solution.py:23
  99.2 6.0 %collective-permute-start.12 = (f32[1,8,128]{2,1,0:T(8,128)S(1)}, f32[1,8,128]{2,1,0:T(8,128)S(1)}, u32[]{:S(2)}, u32[]{:S(2)}) collective-permute-start(f32[1,8,128]{2,1,0:T(8,128)S(1)} %get-tuple-element.54), channel_id=1, source_target_pairs={{16,0},{17,1},{18,2},{19,3},{20,4},{21,5},{22,6},{23,7},{24,8},{25... | collective-permute-start | bytes 12296 | tf_op jit(solution)/shard_map/ppermute | solution.py:26
  105.2 6.6 %collective-permute-start.14 = (f32[18,1,128]{2,1,0:T(1,128)S(1)}, f32[18,1,128]{2,1,0:T(1,128)S(1)}, u32[]{:S(2)}, u32[]{:S(2)}) collective-permute-start(f32[18,1,128]{2,1,0:T(1,128)S(1)} %get-tuple-element.44), channel_id=1, source_target_pairs={{4,0},{8,4},{12,8},{5,1},{9,5},{13,9},{6,2},{10,6},{14,10},{7,3},{... | collective-permute-start | bytes 27656 | tf_op jit(solution)/shard_map/ppermute | solution.py:26
  112.7 15.4 %collective-permute-start.16 = (f32[18,10,1]{2,1,0:T(8,128)}, f32[18,10,1]{2,1,0:T(8,128)}, u32[]{:S(2)}, u32[]{:S(2)}) collective-permute-start(f32[18,10,1]{2,1,0:T(8,128)} %get-tuple-element.33), channel_id=1, source_target_pairs={{1,0},{2,1},{3,2},{5,4},{6,5},{7,6},{9,8},{10,9},{11,10},{13,12},{... | collective-permute-start | bytes 2168 | tf_op jit(solution)/shard_map/ppermute | solution.py:26
  113.9 14.1 %collective-permute-start.17 = (f32[18,10,1]{2,1,0:T(8,128)}, f32[18,10,1]{2,1,0:T(8,128)}, u32[]{:S(2)}, u32[]{:S(2)}) collective-permute-start(f32[18,10,1]{2,1,0:T(8,128)} %get-tuple-element.34), channel_id=1, source_target_pairs={{0,1},{1,2},{2,3},{4,5},{5,6},{6,7},{8,9},{9,10},{10,11},{12,13},{... | collective-permute-start | bytes 2168 | tf_op jit(solution)/shard_map/ppermute | solution.py:23
  137.5 6.0 %collective-permute-start.18 = (f32[1,4,64]{2,1,0:T(4,128)S(1)}, f32[1,4,64]{2,1,0:T(4,128)S(1)}, u32[]{:S(2)}, u32[]{:S(2)}) collective-permute-start(f32[1,4,64]{2,1,0:T(4,128)S(1)} %get-tuple-element.88), channel_id=1, source_target_pairs={{16,0},{17,1},{18,2},{19,3},{20,4},{21,5},{22,6},{23,7},{24,8},{25... | collective-permute-start | bytes 3080 | tf_op jit(solution)/shard_map/ppermute | solution.py:26
  143.5 8.3 %collective-permute-start.20 = (f32[10,1,64]{2,1,0:T(1,128)S(1)}, f32[10,1,64]{2,1,0:T(1,128)S(1)}, u32[]{:S(2)}, u32[]{:S(2)}) collective-permute-start(f32[10,1,64]{2,1,0:T(1,128)S(1)} %get-tuple-element.72), channel_id=1, source_target_pairs={{4,0},{8,4},{12,8},{5,1},{9,5},{13,9},{6,2},{10,6},{14,10},{7,3},{... | collective-permute-start | bytes 7688 | tf_op jit(solution)/shard_map/ppermute | solution.py:26
  164.5 9.1 %collective-permute-start.26 = (f32[10,1,64]{2,1,0:T(1,128)S(1)}, f32[10,1,64]{2,1,0:T(1,128)S(1)}, u32[]{:S(2)}, u32[]{:S(2)}) collective-permute-start(f32[10,1,64]{2,1,0:T(1,128)S(1)} %get-tuple-element.70), channel_id=1, source_target_pairs={{4,0},{8,4},{12,8},{5,1},{9,5},{13,9},{6,2},{10,6},{14,10},{7,3},{... | collective-permute-start | bytes 7688 | tf_op jit(solution)/shard_map/ppermute | solution.py:26
  166.5 7.2 %collective-permute-start.27 = (f32[10,1,64]{2,1,0:T(1,128)S(1)}, f32[10,1,64]{2,1,0:T(1,128)S(1)}, u32[]{:S(2)}, u32[]{:S(2)}) collective-permute-start(f32[10,1,64]{2,1,0:T(1,128)S(1)} %get-tuple-element.69), channel_id=1, source_target_pairs={{0,4},{4,8},{8,12},{1,5},{5,9},{9,13},{2,6},{6,10},{10,14},{3,7},{... | collective-permute-start | bytes 7688 | tf_op jit(solution)/shard_map/ppermute | solution.py:23
  173.8 6.1 %collective-permute-start.28 = (f32[10,6,1]{2,1,0:T(8,128)S(1)}, f32[10,6,1]{2,1,0:T(8,128)S(1)}, u32[]{:S(2)}, u32[]{:S(2)}) collective-permute-start(f32[10,6,1]{2,1,0:T(8,128)S(1)} %get-tuple-element.61), channel_id=1, source_target_pairs={{1,0},{2,1},{3,2},{5,4},{6,5},{7,6},{9,8},{10,9},{11,10},{13,12},{... | collective-permute-start | bytes 728 | tf_op jit(solution)/shard_map/ppermute | solution.py:26
  187.7 8.3 %collective-permute-start.32 = (f32[6,1,32]{2,0,1:T(8,128)S(1)}, f32[6,1,32]{2,0,1:T(8,128)S(1)}, u32[]{:S(2)}, u32[]{:S(2)}) collective-permute-start(f32[6,1,32]{2,0,1:T(8,128)S(1)} %get-tuple-element.96), channel_id=1, source_target_pairs={{4,0},{8,4},{12,8},{5,1},{9,5},{13,9},{6,2},{10,6},{14,10},{7,3},{... | collective-permute-start | bytes 2312 | tf_op jit(solution)/shard_map/ppermute | solution.py:26
  189.6 6.9 %collective-permute-start.33 = (f32[6,1,32]{2,0,1:T(8,128)S(1)}, f32[6,1,32]{2,0,1:T(8,128)S(1)}, u32[]{:S(2)}, u32[]{:S(2)}) collective-permute-start(f32[6,1,32]{2,0,1:T(8,128)S(1)} %get-tuple-element.95), channel_id=1, source_target_pairs={{0,4},{4,8},{8,12},{1,5},{5,9},{9,13},{2,6},{6,10},{10,14},{3,7},{... | collective-permute-start | bytes 2312 | tf_op jit(solution)/shard_map/ppermute | solution.py:23
  196.6 5.9 %collective-permute-start.34 = (f32[6,4,1]{2,0,1:T(8,128)S(1)}, f32[6,4,1]{2,0,1:T(8,128)S(1)}, u32[]{:S(2)}, u32[]{:S(2)}) collective-permute-start(f32[6,4,1]{2,0,1:T(8,128)S(1)} %get-tuple-element.83), channel_id=1, source_target_pairs={{1,0},{2,1},{3,2},{5,4},{6,5},{7,6},{9,8},{10,9},{11,10},{13,12},{... | collective-permute-start | bytes 296 | tf_op jit(solution)/shard_map/ppermute | solution.py:26
  209.4 9.3 %collective-permute-start.38 = (f32[6,1,32]{2,0,1:T(8,128)S(1)}, f32[6,1,32]{2,0,1:T(8,128)S(1)}, u32[]{:S(2)}, u32[]{:S(2)}) collective-permute-start(f32[6,1,32]{2,0,1:T(8,128)S(1)} %get-tuple-element.94), channel_id=1, source_target_pairs={{4,0},{8,4},{12,8},{5,1},{9,5},{13,9},{6,2},{10,6},{14,10},{7,3},{... | collective-permute-start | bytes 2312 | tf_op jit(solution)/shard_map/ppermute | solution.py:26
  211.4 7.3 %collective-permute-start.39 = (f32[6,1,32]{2,0,1:T(8,128)S(1)}, f32[6,1,32]{2,0,1:T(8,128)S(1)}, u32[]{:S(2)}, u32[]{:S(2)}) collective-permute-start(f32[6,1,32]{2,0,1:T(8,128)S(1)} %get-tuple-element.93), channel_id=1, source_target_pairs={{0,4},{4,8},{8,12},{1,5},{5,9},{9,13},{2,6},{6,10},{10,14},{3,7},{... | collective-permute-start | bytes 2312 | tf_op jit(solution)/shard_map/ppermute | solution.py:23
  218.8 5.8 %collective-permute-start.40 = (f32[6,4,1]{2,0,1:T(8,128)S(1)}, f32[6,4,1]{2,0,1:T(8,128)S(1)}, u32[]{:S(2)}, u32[]{:S(2)}) collective-permute-start(f32[6,4,1]{2,0,1:T(8,128)S(1)} %get-tuple-element.81), channel_id=1, source_target_pairs={{1,0},{2,1},{3,2},{5,4},{6,5},{7,6},{9,8},{10,9},{11,10},{13,12},{... | collective-permute-start | bytes 296 | tf_op jit(solution)/shard_map/ppermute | solution.py:26
  231.9 7.7 %collective-permute-start.44 = (f32[4,1,16]{2,0,1:T(4,128)S(1)}, f32[4,1,16]{2,0,1:T(4,128)S(1)}, u32[]{:S(2)}, u32[]{:S(2)}) collective-permute-start(f32[4,1,16]{2,0,1:T(4,128)S(1)} %pad_maximum_fusion.293), channel_id=1, source_target_pairs={{4,0},{8,4},{12,8},{5,1},{9,5},{13,9},{6,2},{10,6},{14,10},{7,3},{... | collective-permute-start | bytes 776 | tf_op jit(solution)/shard_map/ppermute | solution.py:26
  233.8 6.5 %collective-permute-start.45 = (f32[4,1,16]{2,0,1:T(4,128)S(1)}, f32[4,1,16]{2,0,1:T(4,128)S(1)}, u32[]{:S(2)}, u32[]{:S(2)}) collective-permute-start(f32[4,1,16]{2,0,1:T(4,128)S(1)} %pad_maximum_fusion.293), channel_id=1, source_target_pairs={{0,4},{4,8},{8,12},{1,5},{5,9},{9,13},{2,6},{6,10},{10,14},{3,7},{... | collective-permute-start | bytes 776 | tf_op jit(solution)/shard_map/ppermute | solution.py:23
  240.3 5.8 %collective-permute-start.46 = (f32[4,3,1]{2,0,1:T(4,128)S(1)}, f32[4,3,1]{2,0,1:T(4,128)S(1)}, u32[]{:S(2)}, u32[]{:S(2)}) collective-permute-start(f32[4,3,1]{2,0,1:T(4,128)S(1)} %get-tuple-element.109), channel_id=1, source_target_pairs={{1,0},{2,1},{3,2},{5,4},{6,5},{7,6},{9,8},{10,9},{11,10},{13,12},{... | collective-permute-start | bytes 152 | tf_op jit(solution)/shard_map/ppermute | solution.py:26
  253.0 8.1 %collective-permute-start.50 = (f32[4,1,16]{2,0,1:T(4,128)S(1)}, f32[4,1,16]{2,0,1:T(4,128)S(1)}, u32[]{:S(2)}, u32[]{:S(2)}) collective-permute-start(f32[4,1,16]{2,0,1:T(4,128)S(1)} %pad_maximum_fusion.296), channel_id=1, source_target_pairs={{4,0},{8,4},{12,8},{5,1},{9,5},{13,9},{6,2},{10,6},{14,10},{7,3},{... | collective-permute-start | bytes 776 | tf_op jit(solution)/shard_map/ppermute | solution.py:26
  255.0 6.9 %collective-permute-start.51 = (f32[4,1,16]{2,0,1:T(4,128)S(1)}, f32[4,1,16]{2,0,1:T(4,128)S(1)}, u32[]{:S(2)}, u32[]{:S(2)}) collective-permute-start(f32[4,1,16]{2,0,1:T(4,128)S(1)} %pad_maximum_fusion.296), channel_id=1, source_target_pairs={{0,4},{4,8},{8,12},{1,5},{5,9},{9,13},{2,6},{6,10},{10,14},{3,7},{... | collective-permute-start | bytes 776 | tf_op jit(solution)/shard_map/ppermute | solution.py:23
  261.9 5.8 %collective-permute-start.52 = (f32[4,3,1]{2,0,1:T(4,128)S(1)}, f32[4,3,1]{2,0,1:T(4,128)S(1)}, u32[]{:S(2)}, u32[]{:S(2)}) collective-permute-start(f32[4,3,1]{2,0,1:T(4,128)S(1)} %get-tuple-element.107), channel_id=1, source_target_pairs={{1,0},{2,1},{3,2},{5,4},{6,5},{7,6},{9,8},{10,9},{11,10},{13,12},{... | collective-permute-start | bytes 152 | tf_op jit(solution)/shard_map/ppermute | solution.py:26
  274.6 8.1 %collective-permute-start.56 = (f32[4,1,16]{2,0,1:T(4,128)S(1)}, f32[4,1,16]{2,0,1:T(4,128)S(1)}, u32[]{:S(2)}, u32[]{:S(2)}) collective-permute-start(f32[4,1,16]{2,0,1:T(4,128)S(1)} %pad_maximum_fusion.299), channel_id=1, source_target_pairs={{4,0},{8,4},{12,8},{5,1},{9,5},{13,9},{6,2},{10,6},{14,10},{7,3},{... | collective-permute-start | bytes 776 | tf_op jit(solution)/shard_map/ppermute | solution.py:26
  276.6 6.9 %collective-permute-start.57 = (f32[4,1,16]{2,0,1:T(4,128)S(1)}, f32[4,1,16]{2,0,1:T(4,128)S(1)}, u32[]{:S(2)}, u32[]{:S(2)}) collective-permute-start(f32[4,1,16]{2,0,1:T(4,128)S(1)} %pad_maximum_fusion.299), channel_id=1, source_target_pairs={{0,4},{4,8},{8,12},{1,5},{5,9},{9,13},{2,6},{6,10},{10,14},{3,7},{... | collective-permute-start | bytes 776 | tf_op jit(solution)/shard_map/ppermute | solution.py:23
  296.2 8.1 %collective-permute-start.62 = (f32[4,1,16]{2,0,1:T(4,128)S(1)}, f32[4,1,16]{2,0,1:T(4,128)S(1)}, u32[]{:S(2)}, u32[]{:S(2)}) collective-permute-start(f32[4,1,16]{2,0,1:T(4,128)S(1)} %pad_maximum_fusion.302), channel_id=1, source_target_pairs={{4,0},{8,4},{12,8},{5,1},{9,5},{13,9},{6,2},{10,6},{14,10},{7,3},{... | collective-permute-start | bytes 776 | tf_op jit(solution)/shard_map/ppermute | solution.py:26
  298.1 6.9 %collective-permute-start.63 = (f32[4,1,16]{2,0,1:T(4,128)S(1)}, f32[4,1,16]{2,0,1:T(4,128)S(1)}, u32[]{:S(2)}, u32[]{:S(2)}) collective-permute-start(f32[4,1,16]{2,0,1:T(4,128)S(1)} %pad_maximum_fusion.302), channel_id=1, source_target_pairs={{0,4},{4,8},{8,12},{1,5},{5,9},{9,13},{2,6},{6,10},{10,14},{3,7},{... | collective-permute-start | bytes 776 | tf_op jit(solution)/shard_map/ppermute | solution.py:23
  305.1 5.8 %collective-permute-start.64 = (f32[4,3,1]{2,0,1:T(4,128)S(1)}, f32[4,3,1]{2,0,1:T(4,128)S(1)}, u32[]{:S(2)}, u32[]{:S(2)}) collective-permute-start(f32[4,3,1]{2,0,1:T(4,128)S(1)} %get-tuple-element.103), channel_id=1, source_target_pairs={{1,0},{2,1},{3,2},{5,4},{6,5},{7,6},{9,8},{10,9},{11,10},{13,12},{... | collective-permute-start | bytes 152 | tf_op jit(solution)/shard_map/ppermute | solution.py:26
  317.8 8.1 %collective-permute-start.68 = (f32[4,1,16]{2,0,1:T(4,128)S(1)}, f32[4,1,16]{2,0,1:T(4,128)S(1)}, u32[]{:S(2)}, u32[]{:S(2)}) collective-permute-start(f32[4,1,16]{2,0,1:T(4,128)S(1)} %pad_maximum_fusion.305), channel_id=1, source_target_pairs={{4,0},{8,4},{12,8},{5,1},{9,5},{13,9},{6,2},{10,6},{14,10},{7,3},{... | collective-permute-start | bytes 776 | tf_op jit(solution)/shard_map/ppermute | solution.py:26
  319.7 6.9 %collective-permute-start.69 = (f32[4,1,16]{2,0,1:T(4,128)S(1)}, f32[4,1,16]{2,0,1:T(4,128)S(1)}, u32[]{:S(2)}, u32[]{:S(2)}) collective-permute-start(f32[4,1,16]{2,0,1:T(4,128)S(1)} %pad_maximum_fusion.305), channel_id=1, source_target_pairs={{0,4},{4,8},{8,12},{1,5},{5,9},{9,13},{2,6},{6,10},{10,14},{3,7},{... | collective-permute-start | bytes 776 | tf_op jit(solution)/shard_map/ppermute | solution.py:23
  326.7 5.8 %collective-permute-start.70 = (f32[4,3,1]{2,0,1:T(4,128)S(1)}, f32[4,3,1]{2,0,1:T(4,128)S(1)}, u32[]{:S(2)}, u32[]{:S(2)}) collective-permute-start(f32[4,3,1]{2,0,1:T(4,128)S(1)} %get-tuple-element.101), channel_id=1, source_target_pairs={{1,0},{2,1},{3,2},{5,4},{6,5},{7,6},{9,8},{10,9},{11,10},{13,12},{... | collective-permute-start | bytes 152 | tf_op jit(solution)/shard_map/ppermute | solution.py:26
  339.4 8.1 %collective-permute-start.74 = (f32[4,1,16]{2,0,1:T(4,128)S(1)}, f32[4,1,16]{2,0,1:T(4,128)S(1)}, u32[]{:S(2)}, u32[]{:S(2)}) collective-permute-start(f32[4,1,16]{2,0,1:T(4,128)S(1)} %pad_maximum_fusion.308), channel_id=1, source_target_pairs={{4,0},{8,4},{12,8},{5,1},{9,5},{13,9},{6,2},{10,6},{14,10},{7,3},{... | collective-permute-start | bytes 776 | tf_op jit(solution)/shard_map/ppermute | solution.py:26
  341.3 6.9 %collective-permute-start.75 = (f32[4,1,16]{2,0,1:T(4,128)S(1)}, f32[4,1,16]{2,0,1:T(4,128)S(1)}, u32[]{:S(2)}, u32[]{:S(2)}) collective-permute-start(f32[4,1,16]{2,0,1:T(4,128)S(1)} %pad_maximum_fusion.308), channel_id=1, source_target_pairs={{0,4},{4,8},{8,12},{1,5},{5,9},{9,13},{2,6},{6,10},{10,14},{3,7},{... | collective-permute-start | bytes 776 | tf_op jit(solution)/shard_map/ppermute | solution.py:23
  361.0 8.1 %collective-permute-start.80 = (f32[4,1,16]{2,0,1:T(4,128)S(1)}, f32[4,1,16]{2,0,1:T(4,128)S(1)}, u32[]{:S(2)}, u32[]{:S(2)}) collective-permute-start(f32[4,1,16]{2,0,1:T(4,128)S(1)} %pad_maximum_fusion.311), channel_id=1, source_target_pairs={{4,0},{8,4},{12,8},{5,1},{9,5},{13,9},{6,2},{10,6},{14,10},{7,3},{... | collective-permute-start | bytes 776 | tf_op jit(solution)/shard_map/ppermute | solution.py:26
  362.9 6.9 %collective-permute-start.81 = (f32[4,1,16]{2,0,1:T(4,128)S(1)}, f32[4,1,16]{2,0,1:T(4,128)S(1)}, u32[]{:S(2)}, u32[]{:S(2)}) collective-permute-start(f32[4,1,16]{2,0,1:T(4,128)S(1)} %pad_maximum_fusion.311), channel_id=1, source_target_pairs={{0,4},{4,8},{8,12},{1,5},{5,9},{9,13},{2,6},{6,10},{10,14},{3,7},{... | collective-permute-start | bytes 776 | tf_op jit(solution)/shard_map/ppermute | solution.py:23
  382.8 8.1 %collective-permute-start.86 = (f32[6,1,32]{2,0,1:T(8,128)S(1)}, f32[6,1,32]{2,0,1:T(8,128)S(1)}, u32[]{:S(2)}, u32[]{:S(2)}) collective-permute-start(f32[6,1,32]{2,0,1:T(8,128)S(1)} %get-tuple-element.92), channel_id=1, source_target_pairs={{4,0},{8,4},{12,8},{5,1},{9,5},{13,9},{6,2},{10,6},{14,10},{7,3},{... | collective-permute-start | bytes 2312 | tf_op jit(solution)/shard_map/ppermute | solution.py:26
  384.7 6.9 %collective-permute-start.87 = (f32[6,1,32]{2,0,1:T(8,128)S(1)}, f32[6,1,32]{2,0,1:T(8,128)S(1)}, u32[]{:S(2)}, u32[]{:S(2)}) collective-permute-start(f32[6,1,32]{2,0,1:T(8,128)S(1)} %get-tuple-element.91), channel_id=1, source_target_pairs={{0,4},{4,8},{8,12},{1,5},{5,9},{9,13},{2,6},{6,10},{10,14},{3,7},{... | collective-permute-start | bytes 2312 | tf_op jit(solution)/shard_map/ppermute | solution.py:23
  391.7 5.8 %collective-permute-start.88 = (f32[6,4,1]{2,0,1:T(8,128)S(1)}, f32[6,4,1]{2,0,1:T(8,128)S(1)}, u32[]{:S(2)}, u32[]{:S(2)}) collective-permute-start(f32[6,4,1]{2,0,1:T(8,128)S(1)} %get-tuple-element.79), channel_id=1, source_target_pairs={{1,0},{2,1},{3,2},{5,4},{6,5},{7,6},{9,8},{10,9},{11,10},{13,12},{... | collective-permute-start | bytes 296 | tf_op jit(solution)/shard_map/ppermute | solution.py:26
  404.5 8.1 %collective-permute-start.92 = (f32[6,1,32]{2,0,1:T(8,128)S(1)}, f32[6,1,32]{2,0,1:T(8,128)S(1)}, u32[]{:S(2)}, u32[]{:S(2)}) collective-permute-start(f32[6,1,32]{2,0,1:T(8,128)S(1)} %get-tuple-element.90), channel_id=1, source_target_pairs={{4,0},{8,4},{12,8},{5,1},{9,5},{13,9},{6,2},{10,6},{14,10},{7,3},{... | collective-permute-start | bytes 2312 | tf_op jit(solution)/shard_map/ppermute | solution.py:26
  406.4 6.9 %collective-permute-start.93 = (f32[6,1,32]{2,0,1:T(8,128)S(1)}, f32[6,1,32]{2,0,1:T(8,128)S(1)}, u32[]{:S(2)}, u32[]{:S(2)}) collective-permute-start(f32[6,1,32]{2,0,1:T(8,128)S(1)} %get-tuple-element.89), channel_id=1, source_target_pairs={{0,4},{4,8},{8,12},{1,5},{5,9},{9,13},{2,6},{6,10},{10,14},{3,7},{... | collective-permute-start | bytes 2312 | tf_op jit(solution)/shard_map/ppermute | solution.py:23
  413.4 5.8 %collective-permute-start.94 = (f32[6,4,1]{2,0,1:T(8,128)S(1)}, f32[6,4,1]{2,0,1:T(8,128)S(1)}, u32[]{:S(2)}, u32[]{:S(2)}) collective-permute-start(f32[6,4,1]{2,0,1:T(8,128)S(1)} %get-tuple-element.77), channel_id=1, source_target_pairs={{1,0},{2,1},{3,2},{5,4},{6,5},{7,6},{9,8},{10,9},{11,10},{13,12},{... | collective-permute-start | bytes 296 | tf_op jit(solution)/shard_map/ppermute | solution.py:26
  426.7 8.1 %collective-permute-start.98 = (f32[10,1,64]{2,1,0:T(1,128)S(1)}, f32[10,1,64]{2,1,0:T(1,128)S(1)}, u32[]{:S(2)}, u32[]{:S(2)}) collective-permute-start(f32[10,1,64]{2,1,0:T(1,128)S(1)} %get-tuple-element.68), channel_id=1, source_target_pairs={{4,0},{8,4},{12,8},{5,1},{9,5},{13,9},{6,2},{10,6},{14,10},{7,3},{... | collective-permute-start | bytes 7688 | tf_op jit(solution)/shard_map/ppermute | solution.py:26
  428.6 6.9 %collective-permute-start.99 = (f32[10,1,64]{2,1,0:T(1,128)S(1)}, f32[10,1,64]{2,1,0:T(1,128)S(1)}, u32[]{:S(2)}, u32[]{:S(2)}) collective-permute-start(f32[10,1,64]{2,1,0:T(1,128)S(1)} %get-tuple-element.67), channel_id=1, source_target_pairs={{0,4},{4,8},{8,12},{1,5},{5,9},{9,13},{2,6},{6,10},{10,14},{3,7},{... | collective-permute-start | bytes 7688 | tf_op jit(solution)/shard_map/ppermute | solution.py:23
  435.6 5.9 %collective-permute-start.100 = (f32[10,6,1]{2,1,0:T(8,128)S(1)}, f32[10,6,1]{2,1,0:T(8,128)S(1)}, u32[]{:S(2)}, u32[]{:S(2)}) collective-permute-start(f32[10,6,1]{2,1,0:T(8,128)S(1)} %get-tuple-element.59), channel_id=1, source_target_pairs={{1,0},{2,1},{3,2},{5,4},{6,5},{7,6},{9,8},{10,9},{11,10},{13,12},{... | collective-permute-start | bytes 728 | tf_op jit(solution)/shard_map/ppermute | solution.py:26
  448.7 8.1 %collective-permute-start.104 = (f32[10,1,64]{2,1,0:T(1,128)S(1)}, f32[10,1,64]{2,1,0:T(1,128)S(1)}, u32[]{:S(2)}, u32[]{:S(2)}) collective-permute-start(f32[10,1,64]{2,1,0:T(1,128)S(1)} %get-tuple-element.66), channel_id=1, source_target_pairs={{4,0},{8,4},{12,8},{5,1},{9,5},{13,9},{6,2},{10,6},{14,10},{7,3},{... | collective-permute-start | bytes 7688 | tf_op jit(solution)/shard_map/ppermute | solution.py:26
  450.6 6.9 %collective-permute-start.105 = (f32[10,1,64]{2,1,0:T(1,128)S(1)}, f32[10,1,64]{2,1,0:T(1,128)S(1)}, u32[]{:S(2)}, u32[]{:S(2)}) collective-permute-start(f32[10,1,64]{2,1,0:T(1,128)S(1)} %get-tuple-element.65), channel_id=1, source_target_pairs={{0,4},{4,8},{8,12},{1,5},{5,9},{9,13},{2,6},{6,10},{10,14},{3,7},{... | collective-permute-start | bytes 7688 | tf_op jit(solution)/shard_map/ppermute | solution.py:23
  457.7 5.9 %collective-permute-start.106 = (f32[10,6,1]{2,1,0:T(8,128)S(1)}, f32[10,6,1]{2,1,0:T(8,128)S(1)}, u32[]{:S(2)}, u32[]{:S(2)}) collective-permute-start(f32[10,6,1]{2,1,0:T(8,128)S(1)} %get-tuple-element.57), channel_id=1, source_target_pairs={{1,0},{2,1},{3,2},{5,4},{6,5},{7,6},{9,8},{10,9},{11,10},{13,12},{... | collective-permute-start | bytes 728 | tf_op jit(solution)/shard_map/ppermute | solution.py:26
  477.5 8.1 %collective-permute-start.110 = (f32[18,1,128]{2,1,0:T(1,128)S(1)}, f32[18,1,128]{2,1,0:T(1,128)S(1)}, u32[]{:S(2)}, u32[]{:S(2)}) collective-permute-start(f32[18,1,128]{2,1,0:T(1,128)S(1)} %get-tuple-element.42), channel_id=1, source_target_pairs={{4,0},{8,4},{12,8},{5,1},{9,5},{13,9},{6,2},{10,6},{14,10},{7,3},{... | collective-permute-start | bytes 27656 | tf_op jit(solution)/shard_map/ppermute | solution.py:26
  479.4 7.0 %collective-permute-start.111 = (f32[18,1,128]{2,1,0:T(1,128)S(1)}, f32[18,1,128]{2,1,0:T(1,128)S(1)}, u32[]{:S(2)}, u32[]{:S(2)}) collective-permute-start(f32[18,1,128]{2,1,0:T(1,128)S(1)} %get-tuple-element.41), channel_id=1, source_target_pairs={{0,4},{4,8},{8,12},{1,5},{5,9},{9,13},{2,6},{6,10},{10,14},{3,7},{... | collective-permute-start | bytes 27656 | tf_op jit(solution)/shard_map/ppermute | solution.py:23
  486.5 6.5 %collective-permute-start.112 = (f32[18,10,1]{2,1,0:T(8,128)S(1)}, f32[18,10,1]{2,1,0:T(8,128)S(1)}, u32[]{:S(2)}, u32[]{:S(2)}) collective-permute-start(f32[18,10,1]{2,1,0:T(8,128)S(1)} %get-tuple-element.31), channel_id=1, source_target_pairs={{1,0},{2,1},{3,2},{5,4},{6,5},{7,6},{9,8},{10,9},{11,10},{13,12},{... | collective-permute-start | bytes 2168 | tf_op jit(solution)/shard_map/ppermute | solution.py:26
  487.9 6.8 %collective-permute-start.113 = (f32[18,10,1]{2,1,0:T(8,128)S(1)}, f32[18,10,1]{2,1,0:T(8,128)S(1)}, u32[]{:S(2)}, u32[]{:S(2)}) collective-permute-start(f32[18,10,1]{2,1,0:T(8,128)S(1)} %get-tuple-element.32), channel_id=1, source_target_pairs={{0,1},{1,2},{2,3},{4,5},{5,6},{6,7},{8,9},{9,10},{10,11},{12,13},{... | collective-permute-start | bytes 2168 | tf_op jit(solution)/shard_map/ppermute | solution.py:23
  500.9 8.1 %collective-permute-start.116 = (f32[18,1,128]{2,1,0:T(1,128)S(1)}, f32[18,1,128]{2,1,0:T(1,128)S(1)}, u32[]{:S(2)}, u32[]{:S(2)}) collective-permute-start(f32[18,1,128]{2,1,0:T(1,128)S(1)} %get-tuple-element.40), channel_id=1, source_target_pairs={{4,0},{8,4},{12,8},{5,1},{9,5},{13,9},{6,2},{10,6},{14,10},{7,3},{... | collective-permute-start | bytes 27656 | tf_op jit(solution)/shard_map/ppermute | solution.py:26
  502.8 7.0 %collective-permute-start.117 = (f32[18,1,128]{2,1,0:T(1,128)S(1)}, f32[18,1,128]{2,1,0:T(1,128)S(1)}, u32[]{:S(2)}, u32[]{:S(2)}) collective-permute-start(f32[18,1,128]{2,1,0:T(1,128)S(1)} %get-tuple-element.39), channel_id=1, source_target_pairs={{0,4},{4,8},{8,12},{1,5},{5,9},{9,13},{2,6},{6,10},{10,14},{3,7},{... | collective-permute-start | bytes 27656 | tf_op jit(solution)/shard_map/ppermute | solution.py:23
  509.9 6.6 %collective-permute-start.118 = (f32[18,10,1]{2,1,0:T(8,128)S(1)}, f32[18,10,1]{2,1,0:T(8,128)S(1)}, u32[]{:S(2)}, u32[]{:S(2)}) collective-permute-start(f32[18,10,1]{2,1,0:T(8,128)S(1)} %get-tuple-element.29), channel_id=1, source_target_pairs={{1,0},{2,1},{3,2},{5,4},{6,5},{7,6},{9,8},{10,9},{11,10},{13,12},{... | collective-permute-start | bytes 2168 | tf_op jit(solution)/shard_map/ppermute | solution.py:26
  511.2 6.8 %collective-permute-start.119 = (f32[18,10,1]{2,1,0:T(8,128)S(1)}, f32[18,10,1]{2,1,0:T(8,128)S(1)}, u32[]{:S(2)}, u32[]{:S(2)}) collective-permute-start(f32[18,10,1]{2,1,0:T(8,128)S(1)} %get-tuple-element.30), channel_id=1, source_target_pairs={{0,1},{1,2},{2,3},{4,5},{5,6},{6,7},{8,9},{9,10},{10,11},{12,13},{... | collective-permute-start | bytes 2168 | tf_op jit(solution)/shard_map/ppermute | solution.py:23
  524.3 8.1 %collective-permute-start.122 = (f32[18,1,128]{2,1,0:T(1,128)S(1)}, f32[18,1,128]{2,1,0:T(1,128)S(1)}, u32[]{:S(2)}, u32[]{:S(2)}) collective-permute-start(f32[18,1,128]{2,1,0:T(1,128)S(1)} %get-tuple-element.38), channel_id=1, source_target_pairs={{4,0},{8,4},{12,8},{5,1},{9,5},{13,9},{6,2},{10,6},{14,10},{7,3},{... | collective-permute-start | bytes 27656 | tf_op jit(solution)/shard_map/ppermute | solution.py:26
  526.2 7.0 %collective-permute-start.123 = (f32[18,1,128]{2,1,0:T(1,128)S(1)}, f32[18,1,128]{2,1,0:T(1,128)S(1)}, u32[]{:S(2)}, u32[]{:S(2)}) collective-permute-start(f32[18,1,128]{2,1,0:T(1,128)S(1)} %get-tuple-element.37), channel_id=1, source_target_pairs={{0,4},{4,8},{8,12},{1,5},{5,9},{9,13},{2,6},{6,10},{10,14},{3,7},{... | collective-permute-start | bytes 27656 | tf_op jit(solution)/shard_map/ppermute | solution.py:23
  533.3 6.6 %collective-permute-start.124 = (f32[18,10,1]{2,1,0:T(8,128)S(1)}, f32[18,10,1]{2,1,0:T(8,128)S(1)}, u32[]{:S(2)}, u32[]{:S(2)}) collective-permute-start(f32[18,10,1]{2,1,0:T(8,128)S(1)} %get-tuple-element.27), channel_id=1, source_target_pairs={{1,0},{2,1},{3,2},{5,4},{6,5},{7,6},{9,8},{10,9},{11,10},{13,12},{... | collective-permute-start | bytes 2168 | tf_op jit(solution)/shard_map/ppermute | solution.py:26
  534.6 6.8 %collective-permute-start.125 = (f32[18,10,1]{2,1,0:T(8,128)S(1)}, f32[18,10,1]{2,1,0:T(8,128)S(1)}, u32[]{:S(2)}, u32[]{:S(2)}) collective-permute-start(f32[18,10,1]{2,1,0:T(8,128)S(1)} %get-tuple-element.28), channel_id=1, source_target_pairs={{0,1},{1,2},{2,3},{4,5},{5,6},{6,7},{8,9},{9,10},{10,11},{12,13},{... | collective-permute-start | bytes 2168 | tf_op jit(solution)/shard_map/ppermute | solution.py:23
  (78 other events, 794.7 us)
where the time goes:
time: 550 us; the launch traced here: 543 us
  starting transfers between devices  396 us (72%)
  local copies, waits for them, and re-layouts  62.7 us (11%)
  waiting for transfers between devices  51.7 us (9%)
  other arithmetic  29.3 us (5%)
    ppermute x63, starting transfers between devices, extended(): lax.ppermute(lax.slice_in_dim(block, block.shape[dim] - width, None, axis...  300 us
    ppermute x63, starting transfers between devices, extended(): lax.ppermute(lax.slice_in_dim(block, 0, width, axis=dim), axis, backward)  96 us
    reshape x22, local copies, waits for them, and re-layouts, blocks(): return field.reshape(shape[0] // 2, 2, shape[1] // 2, 2, shape[2] // 2, 2)  49.1 us
    ppermute x63, waiting for transfers between devices, extended(): lax.ppermute(lax.slice_in_dim(block, block.shape[dim] - width, None, axis...  40.8 us
  transfers between devices with their start and end apart: 126, of which 59 were waited for; matrix products, arithmetic and copies ran while one was open for 7% of the time, Pallas kernels for 0%

commit v1 on v0

v1 whole, which is shorter than its diff:
```python
import functools

import jax
import jax.numpy as jnp
from jax import lax
from jax.experimental import pallas as pl
from jax.experimental.pallas import tpu as pltpu
from jax.sharding import PartitionSpec as P

LEVELS = 4
COARSE_SWEEPS = 8
AXES = ("gx", "gy", "gz")

RHO_LIQUID = 1000.0
RHO_GAS = 1.0
MEMBRANE_DROP = 49.0
SIGMA_SHIFT = 0.1
OMEGA = 0.8
TIME_STEP = 0.2

ROUNDS = 4 * (LEVELS - 1) + COARSE_SWEEPS - 1 + 1


def harmonic(a, b):
    return 2.0 * a * b / (a + b)


def iota(shape, dim):
    return lax.broadcasted_iota(jnp.int32, shape, dim)


def roll(v, shift, dim):
    size = v.shape[dim]
    shift = shift % size
    return v if shift == 0 else pltpu.roll(v, shift, dim)


def odd_mask(v, dim, step):
    return (iota(v.shape, dim) // step) % 2 == 1


def pair_sum(v, dim, step):
    return v + jnp.where(odd_mask(v, dim, step), roll(v, step, dim), roll(v, -step, dim))


def take_odd(v, dim, step):
    return jnp.where(odd_mask(v, dim, step), v, roll(v, -step, dim))


def take_even(v, dim, step):
    return jnp.where(odd_mask(v, dim, step), roll(v, step, dim), v)


def halves(v):
    w = v.reshape(v.shape[0] // 2, 2, v.shape[1], v.shape[2])
    return w[:, 0], w[:, 1]


def restrict(v, step):
    a, b = halves(v)
    return pair_sum(pair_sum(a + b, 1, step), 2, step)


def prolong(v):
    n = v.shape[0]
    w = jnp.broadcast_to(v[:, None], (n, 2, v.shape[1], v.shape[2]))
    return w.reshape(2 * n, v.shape[1], v.shape[2])


def pack_z(v, lane):
    n = v.shape[0]
    wide = jnp.broadcast_to(v[:, :, lane : lane + 1], v.shape)
    return jnp.sum(jnp.where(iota(v.shape, 2) == iota(v.shape, 0), wide, 0.0), axis=0)


def unpack_z(tile, n):
    return jnp.stack([jnp.broadcast_to(tile[:, i : i + 1], tile.shape) for i in range(n)])


def up(v, halos, d, step):
    if d == 0:
        return jnp.concatenate([v[1:], halos[0][None]], axis=0)
    size = v.shape[d]
    return jnp.where(iota(v.shape, d) >= size - step, halos[d], roll(v, -step, d))


def down(v, halos, d, step):
    if d == 0:
        return jnp.concatenate([halos[0][None], v[:-1]], axis=0)
    return jnp.where(iota(v.shape, d) < step, halos[d], roll(v, step, d))


def kernel(
    counts, fill, flags, smear, velocity, vel_out, frac_out,
    first_x, first_y, first_z, got_x, got_y, got_z,
    out_x, out_y, out_z, in_x, in_y, in_z,
    tables, sides, open_u, vel_low, frac_ref, frac_up_ref, frac_down_ref,
    first_send, first_recv, send_sem, recv_sem,
):
    nx, ny, nz = fill.shape
    place = [lax.axis_index(a) for a in AXES]
    has_low = [place[d] > 0 for d in range(3)]
    has_high = [place[d] < counts[d] - 1 for d in range(3)]

    for ref in (got_x, got_y, got_z, in_x, in_y, in_z):
        ref[...] = jnp.zeros_like(ref)

    barrier = pltpu.get_barrier_semaphore()
    for d in range(3):
        for there, step in ((has_low[d], -1), (has_high[d], 1)):
            @pl.when(there)
            def _():
                pl.semaphore_signal(
                    barrier, inc=1, device_id={AXES[d]: place[d] + step},
                    device_id_type=pl.DeviceIdType.MESH,
                )
    total = sum(c.astype(jnp.int32) for c in has_low + has_high)
    pl.semaphore_wait(barrier, total)

    sends = []

    def copy(src, dst, ssem, rsem, d, way):
        return pltpu.make_async_remote_copy(
            src_ref=src, dst_ref=dst, send_sem=ssem, recv_sem=rsem,
            device_id={AXES[d]: place[d] + (1 if way == 0 else -1)},
            device_id_type=pl.DeviceIdType.MESH,
        )

    def send(src, dst, ssem, rsem, d, way):
        target = has_high[d] if way == 0 else has_low[d]

        @pl.when(target)
        def _():
            copy(src, dst, ssem, rsem, d, way).start()

        sends.append((src, dst, ssem, rsem, d, way))

    def receive(src, dst, ssem, rsem, d, way):
        source = has_low[d] if way == 0 else has_high[d]

        @pl.when(source)
        def _():
            copy(src, dst, ssem, rsem, d, way).wait_recv()

    filled = fill[...].astype(jnp.float32)
    walled = flags[...].astype(jnp.float32)
    soft = 0.4 * smear[...]
    fraction = filled * (1.0 - soft) + (1.0 - filled) * soft
    density = RHO_GAS + (RHO_LIQUID - RHO_GAS) * fraction
    conductance = 1.0 / (density * (1.0 + MEMBRANE_DROP * walled))
    shape = fraction.shape
    speeds = []
    for d in range(3):
        position = place[d] * shape[d] + iota(shape, d)
        speeds.append(
            velocity[d] * (position < shape[d] * counts[d] - 1).astype(jnp.float32)
        )
        open_u[d] = speeds[d]
    frac_ref[...] = fraction

    firsts, gots = (first_x, first_y, first_z), (got_x, got_y, got_z)
    plan = []
    for d in range(3):
        for way in range(2):
            at = shape[d] - 1 if way == 0 else 0
            items = [conductance, fraction] + ([speeds[d]] if way == 0 else [])
            for k, item in enumerate(items):
                if d == 0:
                    firsts[0][way, k] = item[at]
                elif d == 1:
                    firsts[1][way, k] = item[:, at : at + 1, :]
                else:
                    firsts[2][way, k] = pack_z(item, at)
            many = pl.ds(0, len(items))
            plan.append((
                firsts[d].at[way, many], gots[d].at[way, many],
                first_send.at[2 * d + way], first_recv.at[2 * d + way], d, way,
            ))
            send(*plan[-1])
    for item in plan:
        receive(*item)

    def first_halos(k, way):
        return [got_x[way, k], got_y[way, k], unpack_z(got_z[way, k], nx)]

    cond_low, cond_high = first_halos(0, 0), first_halos(0, 1)
    frac_low, frac_high = first_halos(1, 0), first_halos(1, 1)
    speed_low = first_halos(2, 0)
    upper = [harmonic(conductance, up(conductance, cond_high, d, 1)) for d in range(3)]
    lower = [harmonic(down(conductance, cond_low, d, 1), conductance) for d in range(3)]
    shift = SIGMA_SHIFT * conductance
    change = jnp.zeros(shape, jnp.float32)
    for d in range(3):
        frac_up_ref[d] = up(fraction, frac_high, d, 1)
        frac_down_ref[d] = down(fraction, frac_low, d, 1)
        low = down(speeds[d], speed_low, d, 1)
        vel_low[d] = low
        change = change + (speeds[d] - low)
    sides[0][...] = -change

    for level in range(LEVELS):
        diagonal = shift
        for d in range(3):
            tables[level][d] = upper[d]
            tables[level][3 + d] = lower[d]
            diagonal = diagonal + upper[d] + lower[d]
        tables[level][6] = diagonal
        tables[level][7] = OMEGA / diagonal
        if level < LEVELS - 1:
            s = 1 << level
            (a, b), (c, e) = halves(upper[0]), halves(lower[0])
            upper_x = pair_sum(pair_sum(b, 1, s), 2, s)
            lower_x = pair_sum(pair_sum(c, 1, s), 2, s)
            both = lambda v: sum(halves(v))
            upper_y = pair_sum(take_odd(both(upper[1]), 1, s), 2, s)
            lower_y = pair_sum(take_even(both(lower[1]), 1, s), 2, s)
            upper_z = pair_sum(take_odd(both(upper[2]), 2, s), 1, s)
            lower_z = pair_sum(take_even(both(lower[2]), 2, s), 1, s)
            upper, lower = [upper_x, upper_y, upper_z], [lower_x, lower_y, lower_z]
            shift = restrict(shift, s)

    outs, ins = (out_x, out_y, out_z), (in_x, in_y, in_z)
    count = [0]

    def exchange(v):
        r = count[0]
        count[0] += 1
        n = v.shape[0]
        plan = []
        for d in range(3):
            for way in range(2):
                at = v.shape[d] - 1 if way == 0 else 0
                if d == 0:
                    outs[0][r, way] = v[at]
                    src, dst = out_x.at[r, way], in_x.at[r, way]
                elif d == 1:
                    outs[1][r, way, pl.ds(0, n)] = v[:, at : at + 1, :]
                    src = out_y.at[r, way, pl.ds(0, n)]
                    dst = in_y.at[r, way, pl.ds(0, n)]
                else:
                    outs[2][r, way] = pack_z(v, at)
                    src, dst = out_z.at[r, way], in_z.at[r, way]
                k = 2 * d + way
                plan.append((src, dst, send_sem.at[r, k], recv_sem.at[r, k], d, way))
                send(*plan[-1])
        for item in plan:
            receive(*item)
        return [
            [in_x[r, way], in_y[r, way, pl.ds(0, n)], unpack_z(in_z[r, way], n)]
            for way in range(2)
        ]

    def around(v, level):
        low, high = exchange(v)
        t, s = tables[level], 1 << level
        total = 0.0
        for d in range(3):
            total = total + (t[d] * up(v, high, d, s) + t[3 + d] * down(v, low, d, s))
        return total

    def sweep(v, level):
        t = tables[level]
        return (1.0 - OMEGA) * v + t[7] * (sides[level][...] + around(v, level))

    def cycle(level):
        v = tables[level][7] * sides[level][...]
        if level == LEVELS - 1:
            for _ in range(COARSE_SWEEPS - 1):
                v = sweep(v, level)
            return v
        v = sweep(v, level)
        residual = sides[level][...] - tables[level][6] * v + around(v, level)
        sides[level + 1][...] = restrict(residual, 1 << level)
        v = v + prolong(cycle(level + 1))
        for _ in range(2):
            v = sweep(v, level)
        return v

    pressure = cycle(0)
    low, high = exchange(pressure)
    change = jnp.zeros(shape, jnp.float32)
    fraction = frac_ref[...]
    for d in range(3):
        moved = open_u[d] - tables[0][d] * (up(pressure, high, d, 1) - pressure)
        moved_low = vel_low[d] - tables[0][3 + d] * (pressure - down(pressure, low, d, 1))
        vel_out[d] = moved
        flux = moved * jnp.where(moved > 0, fraction, frac_up_ref[d])
        flux_low = moved_low * jnp.where(moved_low > 0, frac_down_ref[d], fraction)
        change = change + (flux - flux_low)
    frac_out[...] = fraction - TIME_STEP * change

    for src, dst, ssem, rsem, d, way in sends:
        target = has_high[d] if way == 0 else has_low[d]

        @pl.when(target)
        def _():
            copy(src, dst, ssem, rsem, d, way).wait_send()


def body(counts, kernel, *refs):
    (fill, flags, smear, velocity, vel_out, frac_out, *scratch) = refs
    first, scratch = scratch[:12], scratch[12:]
    tables, scratch = scratch[:LEVELS], scratch[LEVELS:]
    sides, scratch = scratch[:LEVELS], scratch[LEVELS:]
    kernel(
        counts, fill, flags, smear, velocity, vel_out, frac_out,
        *first, tables, sides, *scratch,
    )


def shards(counts, fill_mask, membrane_flags, smear, velocity):
    nx, ny, nz = fill_mask.shape
    f32 = jnp.float32
    vmem = lambda *s: pltpu.VMEM(s, f32)
    first = [vmem(2, 3, ny, nz), vmem(2, 3, nx, 1, nz), vmem(2, 3, ny, nz)] * 2
    rounds = [
        vmem(ROUNDS, 2, ny, nz), vmem(ROUNDS, 2, nx, 1, nz), vmem(ROUNDS, 2, ny, nz)
    ] * 2
    tables = [vmem(8, nx >> l, ny, nz) for l in range(LEVELS)]
    sides = [vmem(nx >> l, ny, nz) for l in range(LEVELS)]
    rest = [vmem(3, nx, ny, nz), vmem(3, nx, ny, nz), vmem(nx, ny, nz)]
    rest += [vmem(3, nx, ny, nz), vmem(3, nx, ny, nz)]
    sems = [pltpu.SemaphoreType.DMA((6,))] * 2 + [pltpu.SemaphoreType.DMA((ROUNDS, 6))] * 2
    whole = pl.BlockSpec(memory_space=pltpu.VMEM)
    return pl.pallas_call(
        functools.partial(body, counts, kernel),
        out_shape=(
            jax.ShapeDtypeStruct(velocity.shape, f32),
            jax.ShapeDtypeStruct(fill_mask.shape, f32),
        ),
        in_specs=[whole] * 4,
        out_specs=(whole, whole),
        scratch_shapes=first + rounds + tables + sides + rest + sems,
        compiler_params=pltpu.CompilerParams(
            collective_id=0, has_side_effects=True, vmem_limit_bytes=32 * 1024 * 1024
        ),
    )(fill_mask, membrane_flags, smear, velocity)


def solution(mesh):
    placed = (P("gx", "gy", "gz"),) * 3 + (P(None, "gx", "gy", "gz"),)
    counts = tuple(mesh.shape[a] for a in AXES)
    return jax.shard_map(
        functools.partial(shards, counts),
        mesh=mesh,
        in_specs=placed,
        out_specs=(P(None, "gx", "gy", "gz"), P("gx", "gy", "gz")),
        check_vma=False,
    )
```

time: 550 us -> 72.1 us (0.13); the launches traced: 543 us -> 71.5 us
  starting transfers between devices: 396 us -> 0 us
  Pallas kernels: 0 us -> 66.1 us
  local copies, waits for them, and re-layouts: 62.7 us -> 4.75 us
  waiting for transfers between devices: 51.7 us -> 0 us
  other arithmetic: 29.3 us -> 0 us
    ppermute x126 -> x0, starting transfers between devices: 396 us -> none  [the longest x63 300 us: extended(): lax.ppermute(lax.slice_in_dim(block, block.shape[dim] - width, None, axis...]
    pallas_call x0 -> x1, Pallas kernels: none -> 66.1 us  [shards(): pl.pallas_call(functools.partial(body, counts, kernel), out_shape=(jax.Sh...]
    reshape x24 -> x0, local copies, waits for them, and re-layouts: 53.4 us -> none  [the longest x22 49.1 us: blocks(): return field.reshape(shape[0] // 2, 2, shape[1] // 2, 2, shape[2] // 2, 2)]
    ppermute x126 -> x0, waiting for transfers between devices: 51.7 us -> none  [the longest x63 40.8 us: extended(): lax.ppermute(lax.slice_in_dim(block, block.shape[dim] - width, None, axis...]
    reduce_sum x25 -> x0, other arithmetic: 16.7 us -> none  [the longest x3 5.4 us: coarsen_tables(): blocks(lower_faces[2])[..., 0].sum(axis=(1, 3))]
  transfers between devices with their start and end apart: 126 -> 0, of which waited for: 59 -> 0; matrix products, arithmetic and copies ran while one was open for 7% -> 0% of each run, Pallas kernels for 0% -> 0%
where the time goes in v1:
time: 72.1 us; the launch traced here: 71.5 us
  Pallas kernels  66.1 us (92%)
  local copies, waits for them, and re-layouts  4.75 us (7%)
    pallas_call x1, Pallas kernels, shards(): pl.pallas_call(functools.partial(body, counts, kernel), out_shape=(jax.Sh...  66.1 us
    unnamed x10, local copies, waits for them, and re-layouts  4.75 us

profile of v1, /device:TPU:1, one launch (start us, length us, event | category | flops | bytes accessed | tf_op | source)
XLA Modules:
  0.0 71.5 jit_solution(3467352141376549278)
XLA Ops:
  0.6 0.0 copy-start
  0.6 0.9 %copy-done = f32[3,16,8,128]{3,2,1,0:T(8,128)S(1)} copy-done((f32[3,16,8,128]{3,2,1,0:T(8,128)S(1)}, f32[3,16,8,128]{3,2,1,0:T(8,128)}, u32[]{:S(2)}) %copy-start) | copy-done | bytes 196632
  1.6 0.0 copy-start.1
  1.6 0.8 %copy-done.1 = s32[16,8,128]{2,1,0:T(8,128)S(1)} copy-done((s32[16,8,128]{2,1,0:T(8,128)S(1)}, s32[16,8,128]{2,1,0:T(8,128)}, u32[]{:S(2)}) %copy-start.1) | copy-done | bytes 65560
  2.4 0.0 copy-start.2
  2.4 0.8 %copy-done.2 = s32[16,8,128]{2,1,0:T(8,128)S(1)} copy-done((s32[16,8,128]{2,1,0:T(8,128)S(1)}, s32[16,8,128]{2,1,0:T(8,128)}, u32[]{:S(2)}) %copy-start.2) | copy-done | bytes 65560
  3.2 0.0 copy-start.3
  3.2 0.8 %copy-done.3 = f32[16,8,128]{2,1,0:T(8,128)S(1)} copy-done((f32[16,8,128]{2,1,0:T(8,128)S(1)}, f32[16,8,128]{2,1,0:T(8,128)}, u32[]{:S(2)}) %copy-start.3) | copy-done | bytes 65560
  4.1 66.1 %shard_map.59 = (f32[3,16,8,128]{3,2,1,0:T(8,128)S(1)}, f32[16,8,128]{2,1,0:T(8,128)S(1)}) custom-call(s32[16,8,128]{2,1,0:T(8,128)S(1)} %copy-done.1, s32[16,8,128]{2,1,0:T(8,128)S(1)} %copy-done.2, f32[16,8,128]{2,1,0:T(8,128)S(1)} %copy-done.3, f32[3,16,8,128]{3,2,1,0:T(8,128)S(1)} %copy-done), custom_call_target="tpu_custom_call" | custom-call | tf_op jit(solution)/shard_map/pallas_call | solution.py:325
  70.2 0.7 copy.8
  70.9 0.6 copy.9
Async XLA Ops:
  0.6 0.9 %copy-start = (f32[3,16,8,128]{3,2,1,0:T(8,128)S(1)}, f32[3,16,8,128]{3,2,1,0:T(8,128)}, u32[]{:S(2)}) copy-start(f32[3,16,8,128]{3,2,1,0:T(8,128)} %refs_3_.1) | copy-start | bytes 589828
  1.6 0.8 %copy-start.1 = (s32[16,8,128]{2,1,0:T(8,128)S(1)}, s32[16,8,128]{2,1,0:T(8,128)}, u32[]{:S(2)}) copy-start(s32[16,8,128]{2,1,0:T(8,128)} %refs_0_.1) | copy-start | bytes 196612
  2.4 0.8 %copy-start.2 = (s32[16,8,128]{2,1,0:T(8,128)S(1)}, s32[16,8,128]{2,1,0:T(8,128)}, u32[]{:S(2)}) copy-start(s32[16,8,128]{2,1,0:T(8,128)} %refs_1_.1) | copy-start | bytes 196612
  3.2 0.8 %copy-start.3 = (f32[16,8,128]{2,1,0:T(8,128)S(1)}, f32[16,8,128]{2,1,0:T(8,128)}, u32[]{:S(2)}) copy-start(f32[16,8,128]{2,1,0:T(8,128)} %refs_2_.1) | copy-start | bytes 196612

commit v2 on v1

--- a/solution.py
+++ b/solution.py
@@ -90,23 +90,125 @@
     return jnp.where(iota(v.shape, d) < step, halos[d], roll(v, step, d))
 
 
+def gathers(counts, shape):
+    return shape == (16, 8, 128) and counts == (2, 4, 4)
+
+
+def compact(f):
+    wide = iota(f.shape, 2) % 4 == iota(f.shape, 0)
+    return jnp.sum(jnp.where(wide, f, 0.0), axis=0)
+
+
+def turned(v, by):
+    return jnp.concatenate([v[by:], v[:by]], axis=0)
+
+
+def dense_up(v, d, s, ny):
+    lane, row = iota(v.shape, 2), iota(v.shape, 1)
+    if d == 0:
+        return jnp.where(lane % 4 + s < 4, roll(v, -s, 2), roll(turned(v, ny), 4 - s, 2))
+    if d == 1:
+        far = turned(v, 1)
+        return far if s == 2 else roll(jnp.where(row >= 4, v, far), 4, 1)
+    near = roll(v, -4 * s, 2)
+    return jnp.where(lane < 128 - 4 * s, near, roll(near, -1, 1))
+
+
+def dense_down(v, d, s, ny):
+    lane, row = iota(v.shape, 2), iota(v.shape, 1)
+    if d == 0:
+        return jnp.where(lane % 4 >= s, roll(v, s, 2), roll(turned(v, -ny), s - 4, 2))
+    if d == 1:
+        far = turned(v, -1)
+        return far if s == 2 else roll(jnp.where(row < 4, v, far), 4, 1)
+    near = roll(v, 4 * s, 2)
+    return jnp.where(lane >= 4 * s, near, roll(near, 1, 1))
+
+
+def dense_tables(upper, shift, s, ny):
+    lower = [dense_down(upper[d], d, s, ny) for d in range(3)]
+    diagonal = shift
+    for d in range(3):
+        diagonal = diagonal + upper[d] + lower[d]
+    return upper + lower + [diagonal, OMEGA / diagonal]
+
+
+def dense_around(v, t, s, ny):
+    total = 0.0
+    for d in range(3):
+        total = total + (t[d] * dense_up(v, d, s, ny) + t[3 + d] * dense_down(v, d, s, ny))
+    return total
+
+
+def dense_sweep(v, rhs, t, s, ny):
+    return (1.0 - OMEGA) * v + t[7] * (rhs + dense_around(v, t, s, ny))
+
+
+def dense_cycle(rhs, fine, coarse, ny):
+    v = fine[7] * rhs
+    v = dense_sweep(v, rhs, fine, 1, ny)
+    residual = rhs - fine[6] * v + dense_around(v, fine, 1, ny)
+    rhs3 = pair_sum(pair_sum(pair_sum(residual, 2, 1), 1, 4), 2, 4)
+    e = coarse[7] * rhs3
+    for _ in range(COARSE_SWEEPS - 1):
+        e = dense_sweep(e, rhs3, coarse, 2, ny)
+    v = v + e
+    for _ in range(2):
+        v = dense_sweep(v, rhs, fine, 1, ny)
+    return v
+
+
+def local_of(tile, gz):
+    own = jnp.where(iota(tile.shape, 0) % 4 == gz, tile, 0.0)
+    own = pair_sum(pair_sum(own, 0, 1), 0, 2)
+    wide = jnp.broadcast_to(own[None], (4,) + own.shape)
+    wide = jnp.where(iota(wide.shape, 2) % 4 == iota(wide.shape, 0), wide, 0.0)
+    return pair_sum(pair_sum(wide, 2, 1), 2, 2)
+
+
 def kernel(
-    counts, fill, flags, smear, velocity, vel_out, frac_out,
+    counts, fill_at, flags_at, smear_at, velocity_at, vel_out, frac_out,
+    fill, flags, smear, velocity, load_sem,
     first_x, first_y, first_z, got_x, got_y, got_z,
     out_x, out_y, out_z, in_x, in_y, in_z,
     tables, sides, open_u, vel_low, frac_ref, frac_up_ref, frac_down_ref,
     first_send, first_recv, send_sem, recv_sem,
+    own_tables, all_tables, own_side, all_side, answer, all_send, all_recv,
 ):
     nx, ny, nz = fill.shape
     place = [lax.axis_index(a) for a in AXES]
     has_low = [place[d] > 0 for d in range(3)]
     has_high = [place[d] < counts[d] - 1 for d in range(3)]
 
+    gather = gathers(counts, fill.shape)
+    loads = [
+        pltpu.make_async_copy(src, dst, load_sem.at[i])
+        for i, (src, dst) in enumerate(
+            zip((fill_at, flags_at, smear_at, velocity_at), (fill, flags, smear, velocity))
+        )
+    ]
+    for load in loads:
+        load.start()
     for ref in (got_x, got_y, got_z, in_x, in_y, in_z):
         ref[...] = jnp.zeros_like(ref)
 
+    offsets = [
+        (i, j, k) for i in range(counts[0]) for j in range(counts[1])
+        for k in range(counts[2]) if (i, j, k) != (0, 0, 0)
+    ]
+
+    def peer(offset, sign):
+        return tuple(
+            lax.rem(place[d] + (counts[d] + sign * offset[d]), counts[d]) for d in range(3)
+        )
+
     barrier = pltpu.get_barrier_semaphore()
-    for d in range(3):
+    for offset in offsets if gather else []:
+        pl.semaphore_signal(
+            barrier, inc=1, device_id=peer(offset, 1),
+            device_id_type=pl.DeviceIdType.MESH,
+        )
+    for d in [] if gather else range(3):
         for there, step in ((has_low[d], -1), (has_high[d], 1)):
             @pl.when(there)
             def _():
@@ -114,8 +216,9 @@
                     barrier, inc=1, device_id={AXES[d]: place[d] + step},
                     device_id_type=pl.DeviceIdType.MESH,
                 )
-    total = sum(c.astype(jnp.int32) for c in has_low + has_high)
-    pl.semaphore_wait(barrier, total)
+    total = len(offsets)
+    if not gather:
+        total = sum(c.astype(jnp.int32) for c in has_low + has_high)
 
     sends = []
 
@@ -142,6 +245,8 @@
         def _():
             copy(src, dst, ssem, rsem, d, way).wait_recv()
 
+    for load in loads:
+        load.wait()
     filled = fill[...].astype(jnp.float32)
     walled = flags[...].astype(jnp.float32)
     soft = 0.4 * smear[...]
@@ -176,7 +281,9 @@
                 firsts[d].at[way, many], gots[d].at[way, many],
                 first_send.at[2 * d + way], first_recv.at[2 * d + way], d, way,
             ))
-            send(*plan[-1])
+    pl.semaphore_wait(barrier, total)
+    for item in plan:
+        send(*item)
     for item in plan:
         receive(*item)
 
@@ -198,7 +305,7 @@
         change = change + (speeds[d] - low)
     sides[0][...] = -change
 
-    for level in range(LEVELS):
+    for level in range(2 if gather else LEVELS):
         diagonal = shift
         for d in range(3):
             tables[level][d] = upper[d]
@@ -222,7 +329,84 @@
     outs, ins = (out_x, out_y, out_z), (in_x, in_y, in_z)
     count = [0]
 
-    def exchange(v):
+    def spread(src, dst_of, k):
+        dst_of(place)[...] = src[...]
+        copies = []
+        for i, offset in enumerate(offsets):
+            copies.append(pltpu.make_async_remote_copy(
+                src_ref=src, dst_ref=dst_of(place),
+                send_sem=all_send.at[k, i], recv_sem=all_recv.at[k, i],
+                device_id=peer(offset, 1), device_id_type=pl.DeviceIdType.MESH,
+            ))
+            copies[-1].start()
+        return copies
+
+    def table_at(p):
+        return all_tables.at[:, p[0] * counts[1] + p[1], :, p[2]]
+
+    def side_at(p):
+        return all_side.at[p[0] * counts[1] + p[1], :, p[2]]
+
+    def collect(dst_of, k):
+        for i, offset in enumerate(offsets):
+            ref = dst_of(peer(offset, -1))
+            pltpu.make_async_remote_copy(
+                src_ref=ref, dst_ref=ref,
+                send_sem=all_send.at[k, i], recv_sem=all_recv.at[k, i],
+                device_id=peer(offset, -1), device_id_type=pl.DeviceIdType.MESH,
+            ).wait_recv()
+
+    def rows(f):
+        tile = compact(f)
+        return [tile[0:1], tile[4:5]]
+
+    spreads = []
+
+    def send_tables():
+        for k, f in enumerate(upper + [shift]):
+            for j, row in enumerate(rows(f)):
+                own_tables[k, j] = row
+        spreads.extend(spread(own_tables, table_at, 0))
+
+    def coarse_solve(residual2):
+        for j, row in enumerate(rows(residual2)):
+            own_side[j] = row
+        spreads.extend(spread(own_side, side_at, 1))
+        collect(table_at, 0)
+        many = counts[0] * counts[1]
+        shaped = lambda w: w.reshape(many, 8, 128)
+        *up2, shift2 = [shaped(all_tables[k]) for k in range(4)]
+        ny = counts[1]
+        y_z = lambda v: pair_sum(pair_sum(v, 1, 4), 2, 4)
+        up3 = [
+            y_z(take_odd(up2[0], 2, 1)),
+            pair_sum(pair_sum(take_odd(up2[1], 1, 4), 2, 1), 2, 4),
+            pair_sum(pair_sum(take_odd(up2[2], 2, 4), 2, 1), 1, 4),
+        ]
+        shift3 = pair_sum(y_z(shift2), 2, 1)
+        fine = dense_tables(up2, shift2, 1, ny)
+        coarse = dense_tables(up3, shift3, 2, ny)
+        collect(side_at, 1)
+        answer[...] = dense_cycle(shaped(all_side[...]), fine, coarse, ny)
+
+    def answer_at(d, step):
+        p = list(place)
+        if d is not None:
+            p[d] = lax.rem(p[d] + (counts[d] + step), counts[d])
+        return local_of(answer[p[0] * counts[1] + p[1]], p[2])
+
+    def corrected(halos, way):
+        step = -1 if way == 0 else 1
+        e = [answer_at(d, step) for d in range(3)]
+        edge = lambda f, d: f.shape[d] - 1 if way == 0 else 0
+        x, y, z = edge(e[0], 0), edge(e[1], 1), edge(e[2], 2)
+        return [
+            halos[0] + e[0][x],
+            halos[1] + prolong(e[1][:, y : y + 1, :]),
+            halos[2] + prolong(jnp.broadcast_to(e[2][:, :, z : z + 1], e[2].shape)),
+        ]
+
+    def exchange(v, meanwhile=None):
         r = count[0]
         count[0] += 1
         n = v.shape[0]
@@ -243,6 +427,8 @@
                 k = 2 * d + way
                 plan.append((src, dst, send_sem.at[r, k], recv_sem.at[r, k], d, way))
                 send(*plan[-1])
+        if meanwhile is not None:
+            meanwhile()
         for item in plan:
             receive(*item)
         return [
@@ -250,17 +436,18 @@
             for way in range(2)
         ]
 
-    def around(v, level):
-        low, high = exchange(v)
+    def around(v, level, halos=None, meanwhile=None):
+        low, high = halos or exchange(v, meanwhile)
         t, s = tables[level], 1 << level
         total = 0.0
         for d in range(3):
             total = total + (t[d] * up(v, high, d, s) + t[3 + d] * down(v, low, d, s))
         return total
 
-    def sweep(v, level):
+    def sweep(v, level, halos=None, meanwhile=None):
         t = tables[level]
-        return (1.0 - OMEGA) * v + t[7] * (sides[level][...] + around(v, level))
+        total = sides[level][...] + around(v, level, halos, meanwhile)
+        return (1.0 - OMEGA) * v + t[7] * total
 
     def cycle(level):
         v = tables[level][7] * sides[level][...]
@@ -268,8 +455,14 @@
             for _ in range(COARSE_SWEEPS - 1):
                 v = sweep(v, level)
             return v
-        v = sweep(v, level)
-        residual = sides[level][...] - tables[level][6] * v + around(v, level)
+        v = sweep(v, level, None, send_tables if gather and level == 0 else None)
+        halos = exchange(v)
+        residual = sides[level][...] - tables[level][6] * v + around(v, level, halos)
+        if gather and level == 1:
+            coarse_solve(restrict(residual, 1 << level))
+            v = v + prolong(answer_at(None, 0))
+            v = sweep(v, level, [corrected(halos[0], 0), corrected(halos[1], 1)])
+            return sweep(v, level)
         sides[level + 1][...] = restrict(residual, 1 << level)
         v = v + prolong(cycle(level + 1))
         for _ in range(2):
@@ -296,14 +489,18 @@
         def _():
             copy(src, dst, ssem, rsem, d, way).wait_send()
 
+    for item in spreads:
+        item.wait_send()
+
 
 def body(counts, kernel, *refs):
     (fill, flags, smear, velocity, vel_out, frac_out, *scratch) = refs
+    loaded, scratch = scratch[:5], scratch[5:]
     first, scratch = scratch[:12], scratch[12:]
     tables, scratch = scratch[:LEVELS], scratch[LEVELS:]
     sides, scratch = scratch[:LEVELS], scratch[LEVELS:]
     kernel(
-        counts, fill, flags, smear, velocity, vel_out, frac_out,
+        counts, fill, flags, smear, velocity, vel_out, frac_out, *loaded,
         *first, tables, sides, *scratch,
     )
 
@@ -321,16 +518,25 @@
     rest = [vmem(3, nx, ny, nz), vmem(3, nx, ny, nz), vmem(nx, ny, nz)]
     rest += [vmem(3, nx, ny, nz), vmem(3, nx, ny, nz)]
     sems = [pltpu.SemaphoreType.DMA((6,))] * 2 + [pltpu.SemaphoreType.DMA((ROUNDS, 6))] * 2
+    loaded = [pltpu.VMEM(a.shape, a.dtype) for a in (fill_mask, membrane_flags, smear, velocity)]
+    loaded += [pltpu.SemaphoreType.DMA((4,))]
+    many = counts[0] * counts[1]
+    peers = many * counts[2] if gathers(counts, fill_mask.shape) else 1
+    sems += [
+        vmem(4, 2, 1, nz), vmem(4, many, 2, counts[2], 1, nz), vmem(2, 1, nz),
+        vmem(many, 2, counts[2], 1, nz), vmem(many, ny, nz),
+    ] + [pltpu.SemaphoreType.DMA((2, peers))] * 2
     whole = pl.BlockSpec(memory_space=pltpu.VMEM)
+    left = pl.BlockSpec(memory_space=pl.ANY)
     return pl.pallas_call(
         functools.partial(body, counts, kernel),
         out_shape=(
             jax.ShapeDtypeStruct(velocity.shape, f32),
             jax.ShapeDtypeStruct(fill_mask.shape, f32),
         ),
-        in_specs=[whole] * 4,
+        in_specs=[left] * 4,
         out_specs=(whole, whole),
-        scratch_shapes=first + rounds + tables + sides + rest + sems,
+        scratch_shapes=loaded + first + rounds + tables + sides + rest + sems,
         compiler_params=pltpu.CompilerParams(
             collective_id=0, has_side_effects=True, vmem_limit_bytes=32 * 1024 * 1024
         ),

time: 72.1 us -> 48.6 us (0.67)
  Pallas kernels: 66.1 us -> 42.6 us
    pallas_call x1, Pallas kernels: 66.1 us -> 42.6 us  [shards(): pl.pallas_call(functools.partial(body, counts, kernel), out_shape=(jax.Sh...]
where the time goes in v2:
time: 48.6 us; the launch traced here: 48 us
  Pallas kernels  42.6 us (88%)
  local copies, waits for them, and re-layouts  4.75 us (10%)
  between operations  0.65 us (1%)
    pallas_call x1, Pallas kernels, shards(): pl.pallas_call(functools.partial(body, counts, kernel), out_shape=(jax.Sh...  42.6 us
    unnamed x10, local copies, waits for them, and re-layouts  4.75 us

profile of v2, /device:TPU:1, one launch (start us, length us, event | category | flops | bytes accessed | tf_op | source)
XLA Modules:
  0.0 48.0 jit_solution(10345025189181172076)
XLA Ops:
  0.6 0.0 copy-start
  0.6 0.9 %copy-done = f32[3,16,8,128]{3,2,1,0:T(8,128)S(1)} copy-done((f32[3,16,8,128]{3,2,1,0:T(8,128)S(1)}, f32[3,16,8,128]{3,2,1,0:T(8,128)}, u32[]{:S(2)}) %copy-start) | copy-done | bytes 196632
  1.6 0.0 copy-start.1
  1.6 0.8 %copy-done.1 = s32[16,8,128]{2,1,0:T(8,128)S(1)} copy-done((s32[16,8,128]{2,1,0:T(8,128)S(1)}, s32[16,8,128]{2,1,0:T(8,128)}, u32[]{:S(2)}) %copy-start.1) | copy-done | bytes 65560
  2.4 0.0 copy-start.2
  2.4 0.8 %copy-done.2 = s32[16,8,128]{2,1,0:T(8,128)S(1)} copy-done((s32[16,8,128]{2,1,0:T(8,128)S(1)}, s32[16,8,128]{2,1,0:T(8,128)}, u32[]{:S(2)}) %copy-start.2) | copy-done | bytes 65560
  3.2 0.0 copy-start.3
  3.2 0.8 %copy-done.3 = f32[16,8,128]{2,1,0:T(8,128)S(1)} copy-done((f32[16,8,128]{2,1,0:T(8,128)S(1)}, f32[16,8,128]{2,1,0:T(8,128)}, u32[]{:S(2)}) %copy-start.3) | copy-done | bytes 65560
  4.1 42.6 %shard_map.59 = (f32[3,16,8,128]{3,2,1,0:T(8,128)S(1)}, f32[16,8,128]{2,1,0:T(8,128)S(1)}) custom-call(s32[16,8,128]{2,1,0:T(8,128)S(1)} %copy-done.1, s32[16,8,128]{2,1,0:T(8,128)S(1)} %copy-done.2, f32[16,8,128]{2,1,0:T(8,128)S(1)} %copy-done.3, f32[3,16,8,128]{3,2,1,0:T(8,128)S(1)} %copy-done), custom_call_target="tpu_custom_call" | custom-call | tf_op jit(solution)/shard_map/pallas_call | solution.py:531
  46.7 0.7 %copy.8 = f32[3,16,8,128]{3,2,1,0:T(8,128)} copy(f32[3,16,8,128]{3,2,1,0:T(8,128)S(1)} %get-tuple-element.4) | data formatting | bytes 393216
  47.4 0.6 %copy.9 = f32[16,8,128]{2,1,0:T(8,128)} copy(f32[16,8,128]{2,1,0:T(8,128)S(1)} %get-tuple-element.5) | data formatting | bytes 131072
Async XLA Ops:
  0.6 0.9 %copy-start = (f32[3,16,8,128]{3,2,1,0:T(8,128)S(1)}, f32[3,16,8,128]{3,2,1,0:T(8,128)}, u32[]{:S(2)}) copy-start(f32[3,16,8,128]{3,2,1,0:T(8,128)} %refs_3_.1) | copy-start | bytes 589828
  1.6 0.8 %copy-start.1 = (s32[16,8,128]{2,1,0:T(8,128)S(1)}, s32[16,8,128]{2,1,0:T(8,128)}, u32[]{:S(2)}) copy-start(s32[16,8,128]{2,1,0:T(8,128)} %refs_0_.1) | copy-start | bytes 196612
  2.4 0.8 %copy-start.2 = (s32[16,8,128]{2,1,0:T(8,128)S(1)}, s32[16,8,128]{2,1,0:T(8,128)}, u32[]{:S(2)}) copy-start(s32[16,8,128]{2,1,0:T(8,128)} %refs_1_.1) | copy-start | bytes 196612
  3.2 0.8 %copy-start.3 = (f32[16,8,128]{2,1,0:T(8,128)S(1)}, f32[16,8,128]{2,1,0:T(8,128)}, u32[]{:S(2)}) copy-start(f32[16,8,128]{2,1,0:T(8,128)} %refs_2_.1) | copy-start | bytes 196612

commit v3 on v2

--- a/solution.py
+++ b/solution.py
@@ -196,6 +196,7 @@
         (i, j, k) for i in range(counts[0]) for j in range(counts[1])
         for k in range(counts[2]) if (i, j, k) != (0, 0, 0)
     ]
+    offsets.sort(key=lambda o: -sum(max(p, c - p) for p, c in zip(o, counts) if p))
 
     def peer(offset, sign):
         return tuple(
@@ -436,13 +437,40 @@
             for way in range(2)
         ]
 
-    def around(v, level, halos=None, meanwhile=None):
-        low, high = halos or exchange(v, meanwhile)
+    def inside(v, level):
+        t, s = tables[level], 1 << level
+        zero = [jnp.zeros(v.shape[1:], v.dtype), 0.0, 0.0]
+        total = 0.0
+        for d in range(3):
+            total = total + (t[d] * up(v, zero, d, s) + t[3 + d] * down(v, zero, d, s))
+        return total
+
+    def outside(v, level, halos):
+        low, high = halos
         t, s = tables[level], 1 << level
         total = 0.0
-        for d in range(3):
-            total = total + (t[d] * up(v, high, d, s) + t[3 + d] * down(v, low, d, s))
-        return total
+        for d in (1, 2):
+            place_in = iota(v.shape, d)
+            total = total + jnp.where(place_in >= v.shape[d] - s, t[d] * high[d], 0.0)
+            total = total + jnp.where(place_in < s, t[3 + d] * low[d], 0.0)
+        first, last = t[3, 0] * low[0], t[0, v.shape[0] - 1] * high[0]
+        parts = [total[:1] + first[None], total[-1:] + last[None]]
+        if v.shape[0] > 2:
+            parts.insert(1, total[1:-1])
+        return jnp.concatenate(parts, axis=0)
+
+    def around(v, level, halos=None, meanwhile=None):
+        if halos is None:
+            box = []
+
+            def work():
+                if meanwhile is not None:
+                    meanwhile()
+                box.append(inside(v, level))
+
+            halos = exchange(v, work)
+            return box[0] + outside(v, level, halos)
+        return inside(v, level) + outside(v, level, halos)
 
     def sweep(v, level, halos=None, meanwhile=None):
         t = tables[level]
@@ -456,8 +484,10 @@
                 v = sweep(v, level)
             return v
         v = sweep(v, level, None, send_tables if gather and level == 0 else None)
-        halos = exchange(v)
-        residual = sides[level][...] - tables[level][6] * v + around(v, level, halos)
+        box = []
+        halos = exchange(v, lambda: box.append(inside(v, level)))
+        residual = sides[level][...] - tables[level][6] * v
+        residual = residual + (box[0] + outside(v, level, halos))
         if gather and level == 1:
             coarse_solve(restrict(residual, 1 << level))
             v = v + prolong(answer_at(None, 0))
@@ -538,7 +568,7 @@
         out_specs=(whole, whole),
         scratch_shapes=loaded + first + rounds + tables + sides + rest + sems,
         compiler_params=pltpu.CompilerParams(
-            collective_id=0, has_side_effects=True, vmem_limit_bytes=32 * 1024 * 1024
+            collective_id=0, has_side_effects=True, vmem_limit_bytes=60 * 1024 * 1024
         ),
     )(fill_mask, membrane_flags, smear, velocity)
 

time: 48.6 us -> 45.8 us (0.942)
  local copies, waits for them, and re-layouts: 4.75 us -> 2.28 us
    unnamed x10 -> x4, local copies, waits for them, and re-layouts: 4.75 us -> 2.28 us
where the time goes in v3:
time: 45.8 us; the launch traced here: 45.6 us
  Pallas kernels  42.7 us (93%)
  local copies, waits for them, and re-layouts  2.28 us (5%)
  between operations  0.65 us (1%)
    pallas_call x1, Pallas kernels, shards(): pl.pallas_call(functools.partial(body, counts, kernel), out_shape=(jax.Sh...  42.7 us
    unnamed x4, local copies, waits for them, and re-layouts  2.28 us

profile of v3, /device:TPU:1, one launch (start us, length us, event | category | flops | bytes accessed | tf_op | source)
XLA Modules:
  0.0 45.6 jit_solution(1259795472986072880)
XLA Ops:
  0.6 42.7 %shard_map.59 = (f32[3,16,8,128]{3,2,1,0:T(8,128)}, f32[16,8,128]{2,1,0:T(8,128)}) custom-call(s32[16,8,128]{2,1,0:T(8,128)} %refs_0_.1, s32[16,8,128]{2,1,0:T(8,128)} %refs_1_.1, f32[16,8,128]{2,1,0:T(8,128)} %refs_2_.1, f32[3,16,8,128]{3,2,1,0:T(8,128)} %refs_3_.1), custom_call_target="tpu_custom_call" | custom-call | tf_op jit(solution)/shard_map/pallas_call | solution.py:561
  43.3 0.0 copy-start
  43.3 1.6 %copy.8 = f32[3,16,8,128]{3,2,1,0:T(8,128)} copy(f32[3,16,8,128]{3,2,1,0:T(8,128)} %get-tuple-element.4) | data formatting | bytes 393216
  45.0 0.0 copy-done
  45.0 0.6 %copy.9 = f32[16,8,128]{2,1,0:T(8,128)} copy(f32[16,8,128]{2,1,0:T(8,128)S(1)} %copy-done) | data formatting | bytes 131072
Async XLA Ops:
  43.3 1.7 %copy-start = (f32[16,8,128]{2,1,0:T(8,128)S(1)}, f32[16,8,128]{2,1,0:T(8,128)}, u32[]{:S(2)}) copy-start(f32[16,8,128]{2,1,0:T(8,128)} %get-tuple-element.5) | copy-start | bytes 196612

commit v4 on v3

--- a/solution.py
+++ b/solution.py
@@ -189,9 +189,6 @@
     ]
     for load in loads:
         load.start()
-    for ref in (got_x, got_y, got_z, in_x, in_y, in_z):
-        ref[...] = jnp.zeros_like(ref)
-
     offsets = [
         (i, j, k) for i in range(counts[0]) for j in range(counts[1])
         for k in range(counts[2]) if (i, j, k) != (0, 0, 0)
@@ -217,6 +214,15 @@
                     barrier, inc=1, device_id={AXES[d]: place[d] + step},
                     device_id_type=pl.DeviceIdType.MESH,
                 )
+    walls = zip((got_x, got_y, got_z), (in_x, in_y, in_z), has_low, has_high)
+    for first_in, all_in, *there in walls:
+        for way in range(2):
+            @pl.when(jnp.logical_not(there[way]))
+            def _():
+                first_in[way] = jnp.zeros(first_in.shape[1:], first_in.dtype)
+                for r in range(all_in.shape[0]):
+                    all_in[r, way] = jnp.zeros(all_in.shape[2:], all_in.dtype)
+
     total = len(offsets)
     if not gather:
         total = sum(c.astype(jnp.int32) for c in has_low + has_high)
@@ -540,14 +546,13 @@
     f32 = jnp.float32
     vmem = lambda *s: pltpu.VMEM(s, f32)
     first = [vmem(2, 3, ny, nz), vmem(2, 3, nx, 1, nz), vmem(2, 3, ny, nz)] * 2
-    rounds = [
-        vmem(ROUNDS, 2, ny, nz), vmem(ROUNDS, 2, nx, 1, nz), vmem(ROUNDS, 2, ny, nz)
-    ] * 2
+    many = 8 if gathers(counts, fill_mask.shape) else ROUNDS
+    rounds = [vmem(many, 2, ny, nz), vmem(many, 2, nx, 1, nz), vmem(many, 2, ny, nz)] * 2
     tables = [vmem(8, nx >> l, ny, nz) for l in range(LEVELS)]
     sides = [vmem(nx >> l, ny, nz) for l in range(LEVELS)]
     rest = [vmem(3, nx, ny, nz), vmem(3, nx, ny, nz), vmem(nx, ny, nz)]
     rest += [vmem(3, nx, ny, nz), vmem(3, nx, ny, nz)]
-    sems = [pltpu.SemaphoreType.DMA((6,))] * 2 + [pltpu.SemaphoreType.DMA((ROUNDS, 6))] * 2
+    sems = [pltpu.SemaphoreType.DMA((6,))] * 2 + [pltpu.SemaphoreType.DMA((many, 6))] * 2
     loaded = [pltpu.VMEM(a.shape, a.dtype) for a in (fill_mask, membrane_flags, smear, velocity)]
     loaded += [pltpu.SemaphoreType.DMA((4,))]
     many = counts[0] * counts[1]

time: 45.8 us -> 44.4 us (0.969)
  Pallas kernels: 42.7 us -> 41.3 us
    pallas_call x1, Pallas kernels: 42.7 us -> 41.3 us  [shards(): pl.pallas_call(functools.partial(body, counts, kernel), out_shape=(jax.Sh...]
where the time goes in v4:
time: 44.4 us; the launch traced here: 44.3 us
  Pallas kernels  41.3 us (93%)
  local copies, waits for them, and re-layouts  2.28 us (5%)
  between operations  0.65 us (1%)
    pallas_call x1, Pallas kernels, shards(): pl.pallas_call(functools.partial(body, counts, kernel), out_shape=(jax.Sh...  41.3 us
    unnamed x4, local copies, waits for them, and re-layouts  2.28 us

profile of v4, /device:TPU:1, one launch (start us, length us, event | category | flops | bytes accessed | tf_op | source)
XLA Modules:
  0.0 44.3 jit_solution(437918242415845614)
XLA Ops:
  0.6 41.3 %shard_map.59 = (f32[3,16,8,128]{3,2,1,0:T(8,128)}, f32[16,8,128]{2,1,0:T(8,128)}) custom-call(s32[16,8,128]{2,1,0:T(8,128)} %refs_0_.1, s32[16,8,128]{2,1,0:T(8,128)} %refs_1_.1, f32[16,8,128]{2,1,0:T(8,128)} %refs_2_.1, f32[3,16,8,128]{3,2,1,0:T(8,128)} %refs_3_.1), custom_call_target="tpu_custom_call" | custom-call | tf_op jit(solution)/shard_map/pallas_call | solution.py:566
  42.0 0.0 copy-start
  42.0 1.6 %copy.8 = f32[3,16,8,128]{3,2,1,0:T(8,128)} copy(f32[3,16,8,128]{3,2,1,0:T(8,128)} %get-tuple-element.4) | data formatting | bytes 393216
  43.6 0.0 copy-done
  43.6 0.6 %copy.9 = f32[16,8,128]{2,1,0:T(8,128)} copy(f32[16,8,128]{2,1,0:T(8,128)S(1)} %copy-done) | data formatting | bytes 131072
Async XLA Ops:
  42.0 1.7 %copy-start = (f32[16,8,128]{2,1,0:T(8,128)S(1)}, f32[16,8,128]{2,1,0:T(8,128)}, u32[]{:S(2)}) copy-start(f32[16,8,128]{2,1,0:T(8,128)} %get-tuple-element.5) | copy-start | bytes 196612

commit v5 on v4

--- a/solution.py
+++ b/solution.py
@@ -168,7 +168,7 @@
 
 def kernel(
     counts, fill_at, flags_at, smear_at, velocity_at, vel_out, frac_out,
-    fill, flags, smear, velocity, load_sem,
+    fill, flags, smear, velocity, load_sem, out_velocity, out_fraction, store_sem,
     first_x, first_y, first_z, got_x, got_y, got_z,
     out_x, out_y, out_z, in_x, in_y, in_z,
     tables, sides, open_u, vel_low, frac_ref, frac_up_ref, frac_down_ref,
@@ -505,6 +505,7 @@
             v = sweep(v, level)
         return v
 
+    stores = []
     pressure = cycle(0)
     low, high = exchange(pressure)
     change = jnp.zeros(shape, jnp.float32)
@@ -512,11 +513,17 @@
     for d in range(3):
         moved = open_u[d] - tables[0][d] * (up(pressure, high, d, 1) - pressure)
         moved_low = vel_low[d] - tables[0][3 + d] * (pressure - down(pressure, low, d, 1))
-        vel_out[d] = moved
+        out_velocity[d] = moved
+        stores.append(
+            pltpu.make_async_copy(out_velocity.at[d], vel_out.at[d], store_sem.at[d])
+        )
+        stores[-1].start()
         flux = moved * jnp.where(moved > 0, fraction, frac_up_ref[d])
         flux_low = moved_low * jnp.where(moved_low > 0, frac_down_ref[d], fraction)
         change = change + (flux - flux_low)
-    frac_out[...] = fraction - TIME_STEP * change
+    out_fraction[...] = fraction - TIME_STEP * change
+    stores.append(pltpu.make_async_copy(out_fraction, frac_out, store_sem.at[3]))
+    stores[-1].start()
 
     for src, dst, ssem, rsem, d, way in sends:
         target = has_high[d] if way == 0 else has_low[d]
@@ -527,11 +534,13 @@
 
     for item in spreads:
         item.wait_send()
+    for item in stores:
+        item.wait()
 
 
 def body(counts, kernel, *refs):
     (fill, flags, smear, velocity, vel_out, frac_out, *scratch) = refs
-    loaded, scratch = scratch[:5], scratch[5:]
+    loaded, scratch = scratch[:8], scratch[8:]
     first, scratch = scratch[:12], scratch[12:]
     tables, scratch = scratch[:LEVELS], scratch[LEVELS:]
     sides, scratch = scratch[:LEVELS], scratch[LEVELS:]
@@ -555,6 +564,7 @@
     sems = [pltpu.SemaphoreType.DMA((6,))] * 2 + [pltpu.SemaphoreType.DMA((many, 6))] * 2
     loaded = [pltpu.VMEM(a.shape, a.dtype) for a in (fill_mask, membrane_flags, smear, velocity)]
     loaded += [pltpu.SemaphoreType.DMA((4,))]
+    loaded += [vmem(*velocity.shape), vmem(*fill_mask.shape), pltpu.SemaphoreType.DMA((4,))]
     many = counts[0] * counts[1]
     peers = many * counts[2] if gathers(counts, fill_mask.shape) else 1
     sems += [
@@ -570,7 +580,7 @@
             jax.ShapeDtypeStruct(fill_mask.shape, f32),
         ),
         in_specs=[left] * 4,
-        out_specs=(whole, whole),
+        out_specs=(left, left),
         scratch_shapes=loaded + first + rounds + tables + sides + rest + sems,
         compiler_params=pltpu.CompilerParams(
             collective_id=0, has_side_effects=True, vmem_limit_bytes=60 * 1024 * 1024

time: 44.4 us -> 44.2 us (level)
  no operation moved by 1% of the time
where the time goes in v5:
time: 44.2 us; the launch traced here: 44.1 us
  Pallas kernels  41.1 us (93%)
  local copies, waits for them, and re-layouts  2.28 us (5%)
  between operations  0.65 us (1%)
    pallas_call x1, Pallas kernels, shards(): pl.pallas_call(functools.partial(body, counts, kernel), out_shape=(jax.Sh...  41.1 us
    unnamed x4, local copies, waits for them, and re-layouts  2.28 us

profile of v5, /device:TPU:1, one launch (start us, length us, event | category | flops | bytes accessed | tf_op | source)
XLA Modules:
  0.0 44.1 jit_solution(9040805433868840491)
XLA Ops:
  0.6 41.1 %shard_map.59 = (f32[3,16,8,128]{3,2,1,0:T(8,128)}, f32[16,8,128]{2,1,0:T(8,128)}) custom-call(s32[16,8,128]{2,1,0:T(8,128)} %refs_0_.1, s32[16,8,128]{2,1,0:T(8,128)} %refs_1_.1, f32[16,8,128]{2,1,0:T(8,128)} %refs_2_.1, f32[3,16,8,128]{3,2,1,0:T(8,128)} %refs_3_.1), custom_call_target="tpu_custom_call" | custom-call | tf_op jit(solution)/shard_map/pallas_call | solution.py:576
  41.8 0.0 copy-start
  41.8 1.6 %copy.8 = f32[3,16,8,128]{3,2,1,0:T(8,128)} copy(f32[3,16,8,128]{3,2,1,0:T(8,128)} %get-tuple-element.4) | data formatting | bytes 393216
  43.4 0.0 copy-done
  43.4 0.6 %copy.9 = f32[16,8,128]{2,1,0:T(8,128)} copy(f32[16,8,128]{2,1,0:T(8,128)S(1)} %copy-done) | data formatting | bytes 131072
Async XLA Ops:
  41.8 1.7 %copy-start = (f32[16,8,128]{2,1,0:T(8,128)S(1)}, f32[16,8,128]{2,1,0:T(8,128)}, u32[]{:S(2)}) copy-start(f32[16,8,128]{2,1,0:T(8,128)} %get-tuple-element.5) | copy-start | bytes 196612
